TPU v7x, 512 devices: a whole 4x8x8 slice. The times are simulated.
512 devices in a mesh: tm: 8 (over y), lat: 16 (over x, z_lo, core), lon: 4 (over z_hi).
Axes of the slice: x: 4, y: 8, z: 8 (z_hi: 4, z_lo: 2; z = z_hi * 2 + z_lo), core: 2. Of those that a mesh axis runs over, the one named last changes fastest.
Arguments:
- increments: float32 [8, 16, 128, 1536], P('tm', None, 'lat', 'lon'), may hold values from -6 to 6
- advection: float32 [16, 128, 1536], P(None, 'lat', 'lon'), may hold values from 0.2 to 0.4
- diffusion: float32 [16, 128, 1536], P(None, 'lat', 'lon'), may hold values from 0.25 to 0.3
- departures: float32 [8, 6, 16, 128, 1536], P('tm', None, None, 'lat', 'lon'), may hold values from -6 to 6
- obs_weight: float32 [16], replicated, may hold values from 0.5 to 2
- error_weight: float32 [16], replicated, may hold values from 0.5 to 2
- penalty_weight: float32 [16], replicated, may hold values from 0.5 to 2
- filter_steps: int32 [24], replicated, may hold values from 0 to 47, as said below
- filter_weights: float32 [24], replicated, may hold values from 0.05 to 0.3
Outputs:
- gradient: float32 [8, 16, 128, 1536], P('tm', None, 'lat', 'lon')
Inputs may be any that keep to these rules, and one draw needn't show every extreme that they name: filter_steps lists, for k = 0 .. 7 in turn, 3 different steps of subwindow k, each in k * 6 to k * 6 + 5.
All inputs are finite; a program needn't handle non-finite values.
Results may differ from a plain program's by a relative error of at most 0.00002.
Values sent between devices are 32-bit elements; how exact they have to be, the bound alone decides.
A program may use at most 64 MiB of HBM per device.

v0:
```python
import jax
import jax.numpy as jnp
from jax import lax
from jax.sharding import PartitionSpec as P


def extended(value, sides, width):
    for axis, dim in sides:
        count, length = (lax.axis_size(axis), value.shape[dim])
        up = [(i, (i + 1) % count) for i in range(count - 1)]
        down = [(j, i) for i, j in up]
        last = lax.slice_in_dim(value, length - width, length, axis=dim)
        initial = lax.slice_in_dim(value, 0, width, axis=dim)
        before = lax.ppermute(last, axis, up)
        after = lax.ppermute(initial, axis, down)
        value = jnp.concatenate([before, value, after], axis=dim)
    return value


def passed_along(value, axis, by):
    count = lax.axis_size(axis)
    return lax.ppermute(value, axis, [(i, (i + by) % count) for i in range(count)])


def from_behind(block, axis, distance):
    devices = range(lax.axis_size(axis))
    route = [(i - distance, i) for i in devices if i - distance in devices]
    return lax.ppermute(block, axis, route)


def split_up(value, dim, count):
    dims = value.shape
    parts = value.reshape(*dims[:dim], count, dims[dim] // count, *dims[dim + 1 :])
    return jnp.moveaxis(parts, dim, 0)


def summed_on_arrival(value, axis, dim):
    parts = split_up(value, dim, lax.axis_size(axis))
    arrived = lax.all_to_all(parts, axis, split_axis=0, concat_axis=0, tiled=True)
    return arrived.sum(axis=0)


def joined_along(parts, dim):
    dims = list(parts.shape[1:])
    dims[dim] *= parts.shape[0]
    return jnp.moveaxis(parts, 0, dim).reshape(dims)


def from_everyone(value, axis):
    copies = jnp.broadcast_to(value, (lax.axis_size(axis), *value.shape))
    return lax.all_to_all(copies, axis, split_axis=0, concat_axis=0, tiled=True)


def collect(value, axis, dim):
    return joined_along(from_everyone(value, axis), dim)


def widen_coefficients(advection, diffusion, width):
    wide_adv, wide_dif = (
        extended(advection, (("lat", 1),), width),
        extended(diffusion, (("lat", 1),), width),
    )
    west_adv, west_dif = passed_along((wide_adv[:, :, -width:], wide_dif[:, :, -width:]), "lon", 1)
    east_adv, east_dif = passed_along((wide_adv[:, :, :width], wide_dif[:, :, :width]), "lon", -1)
    full_adv = jnp.concatenate([west_adv, wide_adv, east_adv], axis=2)
    full_dif = jnp.concatenate([west_dif, wide_dif, east_dif], axis=2)
    return (full_adv, full_dif)


def deep_forward(initial, full_adv, full_dif, inside, width):
    lat_rows = initial.shape[1]
    wide = extended(initial, (("lat", 1),), width)
    edge = passed_along(wide[:, :, -width:], "lon", 1)
    block = jnp.concatenate([edge, wide], axis=2)
    total_rows = block.shape[1]
    fore_adv = full_adv[:, :, :-width]
    fore_dif = full_dif[:, :, :-width]
    states = []
    for level in range(width):
        states.append(block[:, width - level : width - level + lat_rows, width - level :])
        adv_now = fore_adv[:, level + 1 : total_rows - level - 1, level + 1 :]
        dif_now = fore_dif[:, level + 1 : total_rows - level - 1, level + 1 :]
        centre = block[:, 1:-1, 1:]
        western = block[:, 1:-1, :-1]
        meridian = block[:, 2:, 1:] + block[:, :-2, 1:]
        fresh = (1.0 - adv_now - 2.0 * dif_now) * centre + adv_now * western + dif_now * meridian
        block = fresh * inside[level + 1 : total_rows - level - 1][None, :, None]
    return (states, block)


def deep_adjoint(start, forcings, full_adv, full_dif, inside, width):
    stacked = jnp.stack([start] + forcings)
    wide = extended(stacked, (("lat", 2),), width)
    edge = passed_along(wide[:, :, :, :width], "lon", -1)
    block_all = jnp.concatenate([wide, edge], axis=3)
    total_rows = block_all.shape[2]
    total_cols = block_all.shape[3]
    back_adv = full_adv[:, :, width:]
    back_dif = full_dif[:, :, width:]
    adjoint = block_all[0]
    for level in range(1, width + 1):
        section = width - level
        adv_now = back_adv[:, level - 1 : total_rows - level + 1, : total_cols - level + 1]
        dif_now = back_dif[:, level - 1 : total_rows - level + 1, : total_cols - level + 1]
        carried = adv_now * adjoint
        spread = dif_now * adjoint
        keep = (1.0 - adv_now - 2.0 * dif_now)[:, 1:-1, :-1]
        moved = (
            keep * adjoint[:, 1:-1, :-1]
            + carried[:, 1:-1, 1:]
            + (spread[:, 2:, :-1] + spread[:, :-2, :-1])
        )
        forcing = block_all[1 + section][:, level : total_rows - level, : total_cols - level]
        adjoint = (forcing + moved) * inside[level : total_rows - level][None, :, None]
    return adjoint


def body(
    increments,
    advection,
    diffusion,
    departures,
    obs_weight,
    error_weight,
    penalty_weight,
    filter_steps,
    filter_weights,
):
    position = lax.axis_index("tm")
    members = lax.axis_size("tm")
    count_steps = departures.shape[1]
    middle = members * count_steps // 2
    initial = increments[0]
    lat_rows = initial.shape[1]
    following = from_behind(initial, "tm", -1)
    window_steps = position * count_steps + jnp.arange(count_steps, dtype=jnp.int32)
    hits = (filter_steps[None, :] == window_steps[:, None]).astype(jnp.float32)
    tap = jnp.sum(hits * filter_weights[None, :], axis=1)
    coef = tap - (window_steps == middle).astype(jnp.float32)
    obs_level = obs_weight[:, None, None]
    err_level = error_weight[:, None, None]
    full_adv, full_dif = widen_coefficients(advection, diffusion, count_steps)
    global_rows = (
        lax.axis_index("lat") * lat_rows
        - count_steps
        + jnp.arange(lat_rows + 2 * count_steps, dtype=jnp.int32)
    )
    inside = ((global_rows >= 0) & (global_rows < lat_rows * lax.axis_size("lat"))).astype(
        jnp.float32
    )
    states, final = deep_forward(initial, full_adv, full_dif, inside, count_steps)
    partial_value = jnp.zeros(initial.shape, jnp.float32)
    for step in range(count_steps):
        partial_value = partial_value + coef[step] * states[step]
    previous = from_behind(final, "tm", 1)
    mismatch = initial - previous
    scale = jnp.where(position == 0, jnp.ones_like(err_level), err_level)
    share = summed_on_arrival(partial_value, "tm", 0)
    levels = share.shape[0]
    weights_here = lax.dynamic_slice_in_dim(penalty_weight, position * levels, levels)
    force = collect(weights_here[:, None, None] * share, "tm", 0)
    alive = (position < members - 1).astype(jnp.float32)
    adjoint = -(err_level * (following - final)) * alive
    forcings = [
        obs_level * (states[step] - departures[0, step]) + coef[step] * force
        for step in range(count_steps)
    ]
    adjoint = deep_adjoint(adjoint, forcings, full_adv, full_dif, inside, count_steps)
    return (adjoint + scale * mismatch)[None]


def solution(mesh):
    return jax.shard_map(
        body,
        mesh=mesh,
        in_specs=(
            P("tm", None, "lat", "lon"),
            P(None, "lat", "lon"),
            P(None, "lat", "lon"),
            P("tm", None, None, "lat", "lon"),
            P(),
            P(),
            P(),
            P(),
            P(),
        ),
        out_specs=P("tm", None, "lat", "lon"),
        check_vma=False,
    )
```

profile of v0, /device:TPU:10, one launch (start us, length us, event | category | flops | bytes accessed | tf_op | source)
XLA Modules:
  0.0 183.1 jit_solution(6724892120931707360)
XLA Ops:
  0.0 1.1 fusion.72
  1.1 3.8 %collective-permute-start.8 = (f32[16,6,384]{2,1,0:T(8,128)S(1)}, f32[16,6,384]{2,1,0:T(8,128)S(1)}, u32[]{:S(2)}, u32[]{:S(2)}) collective-permute-start(f32[16,6,384]{2,1,0:T(8,128)S(1)} %get-tuple-element.54), channel_id=1, source_target_pairs={{4,0},{8,4},{12,8},{16,12},{20,16},{24,20},{28,24},{32,28},{36,32}... | collective-permute-start | bytes 442376 | tf_op jit(solution)/shard_map/ppermute | solution.py:15
  5.0 1.9 %collective-permute-start.7 = (f32[16,6,384]{2,1,0:T(8,128)S(1)}, f32[16,6,384]{2,1,0:T(8,128)S(1)}, u32[]{:S(2)}, u32[]{:S(2)}) collective-permute-start(f32[16,6,384]{2,1,0:T(8,128)S(1)} %get-tuple-element.53), channel_id=1, source_target_pairs={{0,4},{4,8},{8,12},{12,16},{16,20},{20,24},{24,28},{28,32},{32,36}... | collective-permute-start | bytes 442376 | tf_op jit(solution)/shard_map/ppermute | solution.py:14
  6.9 1.1 fusion.73
  7.9 4.5 %collective-permute-start.5 = (f32[16,6,384]{2,1,0:T(8,128)S(1)}, f32[16,6,384]{2,1,0:T(8,128)S(1)}, u32[]{:S(2)}, u32[]{:S(2)}) collective-permute-start(f32[16,6,384]{2,1,0:T(8,128)S(1)} %get-tuple-element.56), channel_id=1, source_target_pairs={{4,0},{8,4},{12,8},{16,12},{20,16},{24,20},{28,24},{32,28},{36,32}... | collective-permute-start | bytes 442376 | tf_op jit(solution)/shard_map/ppermute | solution.py:15
  12.5 1.9 %collective-permute-start.4 = (f32[16,6,384]{2,1,0:T(8,128)S(1)}, f32[16,6,384]{2,1,0:T(8,128)S(1)}, u32[]{:S(2)}, u32[]{:S(2)}) collective-permute-start(f32[16,6,384]{2,1,0:T(8,128)S(1)} %get-tuple-element.55), channel_id=1, source_target_pairs={{0,4},{4,8},{8,12},{12,16},{16,20},{20,24},{24,28},{28,32},{32,36}... | collective-permute-start | bytes 442376 | tf_op jit(solution)/shard_map/ppermute | solution.py:14
  14.5 4.5 %collective-permute-start.2 = (f32[16,6,384]{2,1,0:T(8,128)S(1)}, f32[16,6,384]{2,1,0:T(8,128)S(1)}, u32[]{:S(2)}, u32[]{:S(2)}) collective-permute-start(f32[16,6,384]{2,1,0:T(8,128)S(1)} %get-tuple-element.52), channel_id=1, source_target_pairs={{4,0},{8,4},{12,8},{16,12},{20,16},{24,20},{28,24},{32,28},{36,32}... | collective-permute-start | bytes 442376 | tf_op jit(solution)/shard_map/ppermute | solution.py:15
  20.3 1.9 %collective-permute-start.1 = (f32[16,6,384]{2,1,0:T(8,128)S(1)}, f32[16,6,384]{2,1,0:T(8,128)S(1)}, u32[]{:S(2)}, u32[]{:S(2)}) collective-permute-start(f32[16,6,384]{2,1,0:T(8,128)S(1)} %get-tuple-element.51), channel_id=1, source_target_pairs={{0,4},{4,8},{8,12},{12,16},{16,20},{20,24},{24,28},{28,32},{32,36}... | collective-permute-start | bytes 442376 | tf_op jit(solution)/shard_map/ppermute | solution.py:14
  22.4 6.1 %collective-permute-start.9 = (f32[16,20,6]{2,1,0:T(8,128)S(1)}, f32[16,20,6]{2,1,0:T(8,128)S(1)}, u32[]{:S(2)}, u32[]{:S(2)}) collective-permute-start(f32[16,20,6]{2,1,0:T(8,128)S(1)} %pad_maximum_fusion.9), channel_id=1, source_target_pairs={{0,1},{1,2},{2,3},{3,0},{4,5},{5,6},{6,7},{7,4},{8,9},{9,10},{10,1... | collective-permute-start | bytes 23048 | tf_op jit(solution)/shard_map/ppermute | solution.py:22
  29.3 6.4 %collective-permute-start.6 = (f32[16,20,6]{2,1,0:T(8,128)S(1)}, f32[16,20,6]{2,1,0:T(8,128)S(1)}, u32[]{:S(2)}, u32[]{:S(2)}) collective-permute-start(f32[16,20,6]{2,1,0:T(8,128)S(1)} %get-tuple-element.43), channel_id=1, source_target_pairs={{0,1},{1,2},{2,3},{3,0},{4,5},{5,6},{6,7},{7,4},{8,9},{9,10},{10,1... | collective-permute-start | bytes 23048 | tf_op jit(solution)/shard_map/ppermute | solution.py:22
  35.9 2.5 %collective-permute-start.13 = (f32[16,20,6]{2,1,0:T(8,128)S(1)}, f32[16,20,6]{2,1,0:T(8,128)S(1)}, u32[]{:S(2)}, u32[]{:S(2)}) collective-permute-start(f32[16,20,6]{2,1,0:T(8,128)S(1)} %get-tuple-element.41), channel_id=1, source_target_pairs={{0,3},{1,0},{2,1},{3,2},{4,7},{5,4},{6,5},{7,6},{8,11},{9,8},{10,9... | collective-permute-start | bytes 23048 | tf_op jit(solution)/shard_map/ppermute | solution.py:22
  38.4 4.3 %collective-permute-start.3 = (f32[16,20,6]{2,1,0:T(8,128)S(1)}, f32[16,20,6]{2,1,0:T(8,128)S(1)}, u32[]{:S(2)}, u32[]{:S(2)}) collective-permute-start(f32[16,20,6]{2,1,0:T(8,128)S(1)} %get-tuple-element.42), channel_id=1, source_target_pairs={{0,1},{1,2},{2,3},{3,0},{4,5},{5,6},{6,7},{7,4},{8,9},{9,10},{10,1... | collective-permute-start | bytes 23048 | tf_op jit(solution)/shard_map/ppermute | solution.py:22
  43.1 8.0 %collective-permute-done.6 = f32[16,20,6]{2,1,0:T(8,128)S(1)} collective-permute-done((f32[16,20,6]{2,1,0:T(8,128)S(1)}, f32[16,20,6]{2,1,0:T(8,128)S(1)}, u32[]{:S(2)}, u32[]{:S(2)}) %collective-permute-start.6) | collective-permute-done | bytes 7712 | tf_op jit(solution)/shard_map/ppermute | solution.py:22
  51.6 5.5 %collective-permute-done.3 = f32[16,20,6]{2,1,0:T(8,128)S(1)} collective-permute-done((f32[16,20,6]{2,1,0:T(8,128)S(1)}, f32[16,20,6]{2,1,0:T(8,128)S(1)}, u32[]{:S(2)}, u32[]{:S(2)}) %collective-permute-start.3) | collective-permute-done | bytes 7712 | tf_op jit(solution)/shard_map/ppermute | solution.py:22
  57.6 1.3 fusion.6
  58.9 0.9 fusion.42
  62.4 4.3 %multiply_add_fusion = f32[16,8,384]{2,1,0:T(8,128)S(1)} fusion(f32[16,12,386]{2,1,0:T(8,128)S(1)} %fusion.34, f32[16,14,387]{2,1,0:T(8,128)S(1)} %fusion.38, f32[16,16,388]{2,1,0:T(8,128)S(1)} %fusion.42, f32[16,18,389]{2,1,0:T(8,128)S(1)} %fusion.6, f32[16,10,385]{2,1,0:T(8,128)S(1)} %fusion.30, f32[]{:T(128)} %bitcast.8, f32[]{:T(128)} %bitcast.7, ...), kind=kLoop, calls=%fused_computation.148 | loop fusion | flops 540672 | bytes 1376280 | tf_op jit(solution)/shard_map/add | solution.py:154
  67.6 7.5 %all-to-all-start = ((f32[8,2,8,384]{3,1,2,0:T(2,128)}), f32[8,2,8,384]{3,1,2,0:T(2,128)S(1)}, u32[]{:S(2)}, u32[]{:S(2)}) async-start(f32[8,2,8,384]{3,1,2,0:T(2,128)} %copy.65), calls=%async_computation | async-start | bytes 393216 | tf_op jit(solution)/shard_map/all_to_all | solution.py:39
  75.1 1.9 %collective-permute-start = (f32[16,8,384]{2,1,0:T(8,128)S(1)}, f32[16,8,384]{2,1,0:T(8,128)}, u32[]{:S(2)}, u32[]{:S(2)}) collective-permute-start(f32[16,8,384]{2,1,0:T(8,128)S(1)} %bitcast.94), channel_id=1, source_target_pairs={{64,0},{128,64},{192,128},{256,192},{320,256},{384,320},{448,384},... | collective-permute-start | bytes 589832 | tf_op jit(solution)/shard_map/ppermute | solution.py:28
  77.1 7.1 %all-to-all-done = f32[8,2,8,384]{3,1,2,0:T(2,128)S(1)} async-done(((f32[8,2,8,384]{3,1,2,0:T(2,128)}), f32[8,2,8,384]{3,1,2,0:T(2,128)S(1)}, u32[]{:S(2)}, u32[]{:S(2)}) %all-to-all-start) | async-done | bytes 196640 | tf_op jit(solution)/shard_map/all_to_all | solution.py:39
  85.1 4.6 %all-to-all-start.1 = ((f32[8,2,8,384]{3,1,2,0:T(2,128)}), f32[8,2,8,384]{3,1,2,0:T(2,128)}, u32[]{:S(2)}, u32[]{:S(2)}) async-start(f32[8,2,8,384]{3,1,2,0:T(2,128)} %broadcast_in_dim.4), calls=%async_computation.1 | async-start | bytes 393216 | tf_op jit(solution)/shard_map/all_to_all | solution.py:51
  89.8 2.6 %bitcast_dynamic-update-slice_fusion.5 = (f32[7,16,8,384]{3,2,1,0:T(8,128)S(1)}, f32[16,8,384]{2,1,0:T(8,128)}) fusion(f32[16,8,384]{2,1,0:T(8,128)} %collective-permute-done, f32[]{:T(128)S(6)} %convert_element_type.11, f32[16]{0:T(128)S(1)} %copy-done.22, f32[8]{0:T(128)S(1)} %slice.446, f32[16,8,384]{2,1,0:T(8,128)} %param.11, ...), kind=kLoop, calls=%fused_computation.147 | loop fusion | flops 688127 | bytes 1769572
  92.4 5.8 %all-to-all-done.1 = f32[8,2,8,384]{3,1,2,0:T(2,128)} async-done(((f32[8,2,8,384]{3,1,2,0:T(2,128)}), f32[8,2,8,384]{3,1,2,0:T(2,128)}, u32[]{:S(2)}, u32[]{:S(2)}) %all-to-all-start.1) | async-done | bytes 196640 | tf_op jit(solution)/shard_map/all_to_all | solution.py:51
  98.1 5.0 %copy_multiply_fusion = (f32[8,2,8,384]{3,2,1,0:T(8,128)S(1)}, f32[8,2,8,384]{3,2,1,0:T(8,128)S(1)}, f32[8,2,8,384]{3,2,1,0:T(8,128)S(1)}, f32[8,2,8,384]{3,2,1,...) fusion(f32[8,2,8,384]{3,1,2,0:T(2,128)} %all-to-all-done.1, f32[]{:T(128)} %bitcast.8, ...), kind=kLoop, calls=%fused_computation.149 | loop fusion | flops 294912 | bytes 1376280 | tf_op jit(solution)/shard_map/mul | solution.py:165
  103.3 1.8 bitcast_add_fusion
  105.7 3.2 %collective-permute-start.11 = (f32[7,16,6,384]{3,1,2,0:T(8,128)S(1)}, f32[7,16,6,384]{3,1,2,0:T(8,128)}, u32[]{:S(2)}, u32[]{:S(2)}) collective-permute-start(f32[7,16,6,384]{3,1,2,0:T(8,128)S(1)} %copy.73), channel_id=1, source_target_pairs={{4,0},{8,4},{12,8},{16,12},{20,16},{24,20},{28,24},{32,28},{36,32}... | collective-permute-start | bytes 3096584 | tf_op jit(solution)/shard_map/ppermute | solution.py:15
  108.9 1.2 copy.72
  110.0 2.1 %collective-permute-start.10 = (f32[7,16,6,384]{3,1,2,0:T(8,128)}, f32[7,16,6,384]{3,1,2,0:T(8,128)}, u32[]{:S(2)}, u32[]{:S(2)}) collective-permute-start(f32[7,16,6,384]{3,1,2,0:T(8,128)} %copy.72), channel_id=1, source_target_pairs={{0,4},{4,8},{8,12},{12,16},{16,20},{20,24},{24,28},{28,32},{32,36}... | collective-permute-start | bytes 3096584 | tf_op jit(solution)/shard_map/ppermute | solution.py:14
  112.1 14.9 %collective-permute-done.11 = f32[7,16,6,384]{3,1,2,0:T(8,128)} collective-permute-done((f32[7,16,6,384]{3,1,2,0:T(8,128)S(1)}, f32[7,16,6,384]{3,1,2,0:T(8,128)}, u32[]{:S(2)}, u32[]{:S(2)}) %collective-permute-start.11) | collective-permute-done | bytes 1032224 | tf_op jit(solution)/shard_map/ppermute | solution.py:15
  127.1 1.6 copy.75
  128.6 12.2 %collective-permute-done.10 = f32[7,16,6,384]{3,1,2,0:T(8,128)} collective-permute-done((f32[7,16,6,384]{3,1,2,0:T(8,128)}, f32[7,16,6,384]{3,1,2,0:T(8,128)}, u32[]{:S(2)}, u32[]{:S(2)}) %collective-permute-start.10) | collective-permute-done | bytes 1032224 | tf_op jit(solution)/shard_map/ppermute | solution.py:14
  140.8 2.7 %copy.74 = f32[7,16,6,384]{3,2,1,0:T(8,128)} copy(f32[7,16,6,384]{3,1,2,0:T(8,128)} %collective-permute-done.10) | data formatting | bytes 2064384 | tf_op jit(solution)/shard_map/ppermute | solution.py:14
  143.5 2.3 %pad_maximum_fusion.1 = f32[7,16,20,6]{3,2,1,0:T(8,128)} fusion(f32[7,16,6,384]{3,2,1,0:T(8,128)S(1)} %copy.75, f32[7,16,8,384]{3,2,1,0:T(8,128)S(1)} %bitcast_dynamic-update-slice_fusion, f32[7,16,6,384]{3,2,1,0:T(8,128)} %copy.74), kind=kLoop, calls=%fused_computation.1 | loop fusion | flops 26880 | bytes 3494400 | tf_op jit(solution)/shard_map/concatenate | solution.py:16
  145.8 2.9 %copy.76 = f32[7,16,20,6]{2,1,3,0:T(8,128)} copy(f32[7,16,20,6]{3,2,1,0:T(8,128)} %pad_maximum_fusion.1) | data formatting | bytes 107520 | tf_op jit(solution)/shard_map/slice | solution.py:94
  148.7 3.0 %collective-permute-start.12 = (f32[7,16,20,6]{2,1,3,0:T(8,128)}, f32[7,16,20,6]{2,1,3,0:T(8,128)}, u32[]{:S(2)}, u32[]{:S(2)}) collective-permute-start(f32[7,16,20,6]{2,1,3,0:T(8,128)} %copy.76), channel_id=1, source_target_pairs={{0,3},{1,0},{2,1},{3,2},{4,7},{5,4},{6,5},{7,6},{8,11},{9,8},{10,9... | collective-permute-start | bytes 161288 | tf_op jit(solution)/shard_map/ppermute | solution.py:22
  151.7 1.1 broadcast_select_fusion
  152.8 2.0 %collective-permute-start.14 = (f32[16,20,6]{2,1,0:T(8,128)}, f32[16,20,6]{2,1,0:T(8,128)}, u32[]{:S(2)}, u32[]{:S(2)}) collective-permute-start(f32[16,20,6]{2,1,0:T(8,128)} %get-tuple-element.44), channel_id=1, source_target_pairs={{0,3},{1,0},{2,1},{3,2},{4,7},{5,4},{6,5},{7,6},{8,11},{9,8},{10,9... | collective-permute-start | bytes 23048 | tf_op jit(solution)/shard_map/ppermute | solution.py:22
  154.8 0.9 slice.583
  156.6 0.9 slice.571
  158.3 2.0 %collective-permute-start.15 = (f32[16,8,384]{2,1,0:T(8,128)}, f32[16,8,384]{2,1,0:T(8,128)}, u32[]{:S(2)}, u32[]{:S(2)}) collective-permute-start(f32[16,8,384]{2,1,0:T(8,128)} %get-tuple-element.16), channel_id=1, source_target_pairs={{0,64},{64,128},{128,192},{192,256},{256,320},{320,384},{384,448},... | collective-permute-start | bytes 589832 | tf_op jit(solution)/shard_map/ppermute | solution.py:28
  160.4 7.6 %collective-permute-done.12 = f32[7,16,20,6]{2,1,3,0:T(8,128)} collective-permute-done((f32[7,16,20,6]{2,1,3,0:T(8,128)}, f32[7,16,20,6]{2,1,3,0:T(8,128)}, u32[]{:S(2)}, u32[]{:S(2)}) %collective-permute-start.12) | collective-permute-done | bytes 53792 | tf_op jit(solution)/shard_map/ppermute | solution.py:22
  168.0 2.8 %copy.77 = f32[7,16,20,6]{3,2,1,0:T(8,128)} copy(f32[7,16,20,6]{2,1,3,0:T(8,128)} %collective-permute-done.12) | data formatting | bytes 107520 | tf_op jit(solution)/shard_map/ppermute | solution.py:22
  170.8 2.7 %pad_maximum_fusion = f32[7,16,20,390]{3,2,1,0:T(8,128)S(1)} fusion(f32[7,16,20,6]{3,2,1,0:T(8,128)} %copy.77, f32[7,16,6,384]{3,2,1,0:T(8,128)S(1)} %copy.75, f32[7,16,8,384]{3,2,1,0:T(8,128)S(1)} %bitcast_dynamic-update-slice_fusion, f32[7,16,6,384]{3,2,1,0:T(8,128)} %copy.74), kind=kLoop, calls=%fused_computation | loop fusion | flops 2620800 | bytes 6988800 | tf_op jit(solution)/shard_map/concatenate | solution.py:95
  173.5 0.9 slice_bitcast_fusion.6
  174.6 1.1 fusion.63
  175.8 1.1 slice_multiply_fusion.32
  176.9 0.9 slice_multiply_fusion.28
  181.2 2.0 %fusion.48 = f32[1,16,8,384]{3,2,1,0:T(8,128)} fusion(f32[16,10,385]{2,1,0:T(8,128)S(1)} %get-tuple-element.5, f32[16,10,385]{2,1,0:T(8,128)S(1)} %get-tuple-element.6, f32[16,10,385]{2,1,0:T(8,128)S(1)} %copy-done.15, f32[16,10,385]{2,1,0:T(8,128)S(1)} %get-tuple-element.31, f32[16,20,390]{2,1,0:T(8,128)S(1)} %get-tuple-element.17, ...), kind=kLoop, calls=%fused_computation.102 | loop fusion | flops 638976 | bytes 2162784 | tf_op jit(solution)/shard_map/broadcast_in_dim | solution.py:169
  (104 shorter events, 14.0 us)
Async XLA Ops:
  0.0 22.2 %copy-start.2 = (f32[1,16,8,384]{3,2,1,0:T(8,128)S(1)}, f32[1,16,8,384]{3,2,1,0:T(8,128)}, u32[]{:S(2)}) copy-start(f32[1,16,8,384]{3,2,1,0:T(8,128)} %param.9) | copy-start | bytes 589828
  0.0 14.4 %copy-start.7 = (f32[16,8,384]{2,1,0:T(8,128)S(1)}, f32[16,8,384]{2,1,0:T(8,128)}, u32[]{:S(2)}) copy-start(f32[16,8,384]{2,1,0:T(8,128)} %param.10) | copy-start | bytes 589828
  0.0 19.0 %copy-start.23 = (f32[24]{0:T(128)S(1)}, f32[24]{0:T(128)}, u32[]{:S(2)}) copy-start(f32[24]{0:T(128)} %param.17) | copy-start | bytes 292
  0.0 19.0 %copy-start.24 = (s32[24]{0:T(128)S(1)}, s32[24]{0:T(128)}, u32[]{:S(2)}) copy-start(s32[24]{0:T(128)} %param.16) | copy-start | bytes 292
  1.1 27.4 %copy-start.4 = (f32[16,8,384]{2,1,0:T(8,128)S(1)}, f32[16,8,384]{2,1,0:T(8,128)}, u32[]{:S(2)}) copy-start(f32[16,8,384]{2,1,0:T(8,128)} %param.11) | copy-start | bytes 589828
  1.1 19.2 %collective-permute-start.8 = (f32[16,6,384]{2,1,0:T(8,128)S(1)}, f32[16,6,384]{2,1,0:T(8,128)S(1)}, u32[]{:S(2)}, u32[]{:S(2)}) collective-permute-start(f32[16,6,384]{2,1,0:T(8,128)S(1)} %get-tuple-element.54), channel_id=1, source_target_pairs={{4,0},{8,4},{12,8},{16,12},{20,16},{24,20},{28,24},{32,28},{36,32}... | collective-permute-start | bytes 442376 | tf_op jit(solution)/shard_map/ppermute | solution.py:15
  5.0 17.3 %collective-permute-start.7 = (f32[16,6,384]{2,1,0:T(8,128)S(1)}, f32[16,6,384]{2,1,0:T(8,128)S(1)}, u32[]{:S(2)}, u32[]{:S(2)}) collective-permute-start(f32[16,6,384]{2,1,0:T(8,128)S(1)} %get-tuple-element.53), channel_id=1, source_target_pairs={{0,4},{4,8},{8,12},{12,16},{16,20},{20,24},{24,28},{28,32},{32,36}... | collective-permute-start | bytes 442376 | tf_op jit(solution)/shard_map/ppermute | solution.py:14
  7.9 20.5 %collective-permute-start.5 = (f32[16,6,384]{2,1,0:T(8,128)S(1)}, f32[16,6,384]{2,1,0:T(8,128)S(1)}, u32[]{:S(2)}, u32[]{:S(2)}) collective-permute-start(f32[16,6,384]{2,1,0:T(8,128)S(1)} %get-tuple-element.56), channel_id=1, source_target_pairs={{4,0},{8,4},{12,8},{16,12},{20,16},{24,20},{28,24},{32,28},{36,32}... | collective-permute-start | bytes 442376 | tf_op jit(solution)/shard_map/ppermute | solution.py:15
  12.5 16.0 %collective-permute-start.4 = (f32[16,6,384]{2,1,0:T(8,128)S(1)}, f32[16,6,384]{2,1,0:T(8,128)S(1)}, u32[]{:S(2)}, u32[]{:S(2)}) collective-permute-start(f32[16,6,384]{2,1,0:T(8,128)S(1)} %get-tuple-element.55), channel_id=1, source_target_pairs={{0,4},{4,8},{8,12},{12,16},{16,20},{20,24},{24,28},{28,32},{32,36}... | collective-permute-start | bytes 442376 | tf_op jit(solution)/shard_map/ppermute | solution.py:14
  14.5 21.3 %collective-permute-start.2 = (f32[16,6,384]{2,1,0:T(8,128)S(1)}, f32[16,6,384]{2,1,0:T(8,128)S(1)}, u32[]{:S(2)}, u32[]{:S(2)}) collective-permute-start(f32[16,6,384]{2,1,0:T(8,128)S(1)} %get-tuple-element.52), channel_id=1, source_target_pairs={{4,0},{8,4},{12,8},{16,12},{20,16},{24,20},{28,24},{32,28},{36,32}... | collective-permute-start | bytes 442376 | tf_op jit(solution)/shard_map/ppermute | solution.py:15
  20.1 38.8 %copy-start.20 = (f32[16]{0:T(128)}, f32[16]{0:T(128)S(1)}, u32[]{:S(2)}) copy-start(f32[16]{0:T(128)S(1)} %slice.426) | copy-start | bytes 196
  20.2 39.6 %copy-start.18 = (f32[14]{0:T(128)}, f32[14]{0:T(128)S(1)}, u32[]{:S(2)}) copy-start(f32[14]{0:T(128)S(1)} %slice.431) | copy-start | bytes 172
  20.3 15.4 %collective-permute-start.1 = (f32[16,6,384]{2,1,0:T(8,128)S(1)}, f32[16,6,384]{2,1,0:T(8,128)S(1)}, u32[]{:S(2)}, u32[]{:S(2)}) collective-permute-start(f32[16,6,384]{2,1,0:T(8,128)S(1)} %get-tuple-element.51), channel_id=1, source_target_pairs={{0,4},{4,8},{8,12},{12,16},{16,20},{20,24},{24,28},{28,32},{32,36}... | collective-permute-start | bytes 442376 | tf_op jit(solution)/shard_map/ppermute | solution.py:14
  22.4 20.3 %collective-permute-start.9 = (f32[16,20,6]{2,1,0:T(8,128)S(1)}, f32[16,20,6]{2,1,0:T(8,128)S(1)}, u32[]{:S(2)}, u32[]{:S(2)}) collective-permute-start(f32[16,20,6]{2,1,0:T(8,128)S(1)} %pad_maximum_fusion.9), channel_id=1, source_target_pairs={{0,1},{1,2},{2,3},{3,0},{4,5},{5,6},{6,7},{7,4},{8,9},{9,10},{10,1... | collective-permute-start | bytes 23048 | tf_op jit(solution)/shard_map/ppermute | solution.py:22
  28.5 22.7 %copy-start.11 = (f32[16,6,384]{2,1,0:T(8,128)}, f32[16,6,384]{2,1,0:T(8,128)S(1)}, u32[]{:S(2)}) copy-start(f32[16,6,384]{2,1,0:T(8,128)S(1)} %collective-permute-done.5) | copy-start | bytes 442372
  28.5 22.6 %copy-start.13 = (f32[16,6,384]{2,1,0:T(8,128)}, f32[16,6,384]{2,1,0:T(8,128)S(1)}, u32[]{:S(2)}) copy-start(f32[16,6,384]{2,1,0:T(8,128)S(1)} %collective-permute-done.4) | copy-start | bytes 442372
  29.3 21.8 %collective-permute-start.6 = (f32[16,20,6]{2,1,0:T(8,128)S(1)}, f32[16,20,6]{2,1,0:T(8,128)S(1)}, u32[]{:S(2)}, u32[]{:S(2)}) collective-permute-start(f32[16,20,6]{2,1,0:T(8,128)S(1)} %get-tuple-element.43), channel_id=1, source_target_pairs={{0,1},{1,2},{2,3},{3,0},{4,5},{5,6},{6,7},{7,4},{8,9},{9,10},{10,1... | collective-permute-start | bytes 23048 | tf_op jit(solution)/shard_map/ppermute | solution.py:22
  35.9 15.7 %collective-permute-start.13 = (f32[16,20,6]{2,1,0:T(8,128)S(1)}, f32[16,20,6]{2,1,0:T(8,128)S(1)}, u32[]{:S(2)}, u32[]{:S(2)}) collective-permute-start(f32[16,20,6]{2,1,0:T(8,128)S(1)} %get-tuple-element.41), channel_id=1, source_target_pairs={{0,3},{1,0},{2,1},{3,2},{4,7},{5,4},{6,5},{7,6},{8,11},{9,8},{10,9... | collective-permute-start | bytes 23048 | tf_op jit(solution)/shard_map/ppermute | solution.py:22
  38.4 18.7 %collective-permute-start.3 = (f32[16,20,6]{2,1,0:T(8,128)S(1)}, f32[16,20,6]{2,1,0:T(8,128)S(1)}, u32[]{:S(2)}, u32[]{:S(2)}) collective-permute-start(f32[16,20,6]{2,1,0:T(8,128)S(1)} %get-tuple-element.42), channel_id=1, source_target_pairs={{0,1},{1,2},{2,3},{3,0},{4,5},{5,6},{6,7},{7,4},{8,9},{9,10},{10,1... | collective-permute-start | bytes 23048 | tf_op jit(solution)/shard_map/ppermute | solution.py:22
  58.9 3.5 %copy-start.1 = (f32[16,18,389]{2,1,0:T(8,128)}, f32[16,18,389]{2,1,0:T(8,128)S(1)}, u32[]{:S(2)}) copy-start(f32[16,18,389]{2,1,0:T(8,128)S(1)} %fusion.6) | copy-start | bytes 1344388
  61.5 0.9 copy-start
  62.4 4.4 %copy-start.6 = (f32[16,10,385]{2,1,0:T(8,128)}, f32[16,10,385]{2,1,0:T(8,128)S(1)}, u32[]{:S(2)}) copy-start(f32[16,10,385]{2,1,0:T(8,128)S(1)} %fusion.30) | copy-start | bytes 739204
  62.4 14.6 %copy-start.26 = (f32[16]{0:T(128)S(1)}, f32[16]{0:T(128)}, u32[]{:S(2)}) copy-start(f32[16]{0:T(128)} %param.15) | copy-start | bytes 196
  62.4 27.3 %copy-start.22 = (f32[16]{0:T(128)S(1)}, f32[16]{0:T(128)}, u32[]{:S(2)}) copy-start(f32[16]{0:T(128)} %param.14) | copy-start | bytes 196
  67.6 16.7 %all-to-all-start = ((f32[8,2,8,384]{3,1,2,0:T(2,128)}), f32[8,2,8,384]{3,1,2,0:T(2,128)S(1)}, u32[]{:S(2)}, u32[]{:S(2)}) async-start(f32[8,2,8,384]{3,1,2,0:T(2,128)} %copy.65), calls=%async_computation | async-start | bytes 393216 | tf_op jit(solution)/shard_map/all_to_all | solution.py:39
  75.1 14.6 %collective-permute-start = (f32[16,8,384]{2,1,0:T(8,128)S(1)}, f32[16,8,384]{2,1,0:T(8,128)}, u32[]{:S(2)}, u32[]{:S(2)}) collective-permute-start(f32[16,8,384]{2,1,0:T(8,128)S(1)} %bitcast.94), channel_id=1, source_target_pairs={{64,0},{128,64},{192,128},{256,192},{320,256},{384,320},{448,384},... | collective-permute-start | bytes 589832 | tf_op jit(solution)/shard_map/ppermute | solution.py:28
  85.1 13.0 %all-to-all-start.1 = ((f32[8,2,8,384]{3,1,2,0:T(2,128)}), f32[8,2,8,384]{3,1,2,0:T(2,128)}, u32[]{:S(2)}, u32[]{:S(2)}) async-start(f32[8,2,8,384]{3,1,2,0:T(2,128)} %broadcast_in_dim.4), calls=%async_computation.1 | async-start | bytes 393216 | tf_op jit(solution)/shard_map/all_to_all | solution.py:51
  89.8 13.4 %copy-start.17 = (f32[16]{0:T(128)S(1)}, f32[16]{0:T(128)}, u32[]{:S(2)}) copy-start(f32[16]{0:T(128)} %param.13) | copy-start | bytes 196
  98.1 5.1 %copy-start.16 = (f32[1,6,16,8,384]{4,3,2,1,0:T(8,128)S(1)}, f32[1,6,16,8,384]{4,3,2,1,0:T(8,128)}, u32[]{:S(2)}) copy-start(f32[1,6,16,8,384]{4,3,2,1,0:T(8,128)} %param.12) | copy-start | bytes 3538948
  105.7 21.4 %collective-permute-start.11 = (f32[7,16,6,384]{3,1,2,0:T(8,128)S(1)}, f32[7,16,6,384]{3,1,2,0:T(8,128)}, u32[]{:S(2)}, u32[]{:S(2)}) collective-permute-start(f32[7,16,6,384]{3,1,2,0:T(8,128)S(1)} %copy.73), channel_id=1, source_target_pairs={{4,0},{8,4},{12,8},{16,12},{20,16},{24,20},{28,24},{32,28},{36,32}... | collective-permute-start | bytes 3096584 | tf_op jit(solution)/shard_map/ppermute | solution.py:15
  110.0 30.8 %collective-permute-start.10 = (f32[7,16,6,384]{3,1,2,0:T(8,128)}, f32[7,16,6,384]{3,1,2,0:T(8,128)}, u32[]{:S(2)}, u32[]{:S(2)}) collective-permute-start(f32[7,16,6,384]{3,1,2,0:T(8,128)} %copy.72), channel_id=1, source_target_pairs={{0,4},{4,8},{8,12},{12,16},{16,20},{20,24},{24,28},{28,32},{32,36}... | collective-permute-start | bytes 3096584 | tf_op jit(solution)/shard_map/ppermute | solution.py:14
  148.7 19.3 %collective-permute-start.12 = (f32[7,16,20,6]{2,1,3,0:T(8,128)}, f32[7,16,20,6]{2,1,3,0:T(8,128)}, u32[]{:S(2)}, u32[]{:S(2)}) collective-permute-start(f32[7,16,20,6]{2,1,3,0:T(8,128)} %copy.76), channel_id=1, source_target_pairs={{0,3},{1,0},{2,1},{3,2},{4,7},{5,4},{6,5},{7,6},{8,11},{9,8},{10,9... | collective-permute-start | bytes 161288 | tf_op jit(solution)/shard_map/ppermute | solution.py:22
  152.8 21.6 %collective-permute-start.14 = (f32[16,20,6]{2,1,0:T(8,128)}, f32[16,20,6]{2,1,0:T(8,128)}, u32[]{:S(2)}, u32[]{:S(2)}) collective-permute-start(f32[16,20,6]{2,1,0:T(8,128)} %get-tuple-element.44), channel_id=1, source_target_pairs={{0,3},{1,0},{2,1},{3,2},{4,7},{5,4},{6,5},{7,6},{8,11},{9,8},{10,9... | collective-permute-start | bytes 23048 | tf_op jit(solution)/shard_map/ppermute | solution.py:22
  158.3 22.5 %collective-permute-start.15 = (f32[16,8,384]{2,1,0:T(8,128)}, f32[16,8,384]{2,1,0:T(8,128)}, u32[]{:S(2)}, u32[]{:S(2)}) collective-permute-start(f32[16,8,384]{2,1,0:T(8,128)} %get-tuple-element.16), channel_id=1, source_target_pairs={{0,64},{64,128},{128,192},{192,256},{256,320},{320,384},{384,448},... | collective-permute-start | bytes 589832 | tf_op jit(solution)/shard_map/ppermute | solution.py:28
  173.5 0.9 copy-start.5
  173.5 1.0 copy-start.12
  173.5 1.1 copy-start.14
  175.8 1.1 copy-start.21
  176.9 1.0 copy-start.10
  176.9 1.0 copy-start.19
  177.9 1.0 copy-start.9
  179.0 1.0 copy-start.8
  180.0 0.9 copy-start.3
  180.0 1.1 copy-start.15
  180.0 1.1 copy-start.25
where the time goes:
time: 185 us; the launch traced here: 183 us
  starting transfers between devices  64.2 us (35%)
  waiting for transfers between devices  61.2 us (33%)
  other arithmetic  35.2 us (19%)
  local copies, waits for them, and re-layouts  22 us (12%)
    ppermute x6, starting transfers between devices, passed_along(): lax.ppermute(value, axis, [(i, (i + by) % count) for i in range(count)])  24.2 us
    ppermute x6, waiting for transfers between devices, passed_along(): lax.ppermute(value, axis, [(i, (i + by) % count) for i in range(count)])  21.2 us
    ppermute x4, starting transfers between devices, extended(): after = lax.ppermute(initial, axis, down)  16.1 us
    ppermute x4, waiting for transfers between devices, extended(): after = lax.ppermute(initial, axis, down)  14.9 us
    ppermute x4, waiting for transfers between devices, extended(): before = lax.ppermute(last, axis, up)  12.2 us
    ppermute x4, starting transfers between devices, extended(): before = lax.ppermute(last, axis, up)  7.84 us
    all_to_all x1, starting transfers between devices, summed_on_arrival(): lax.all_to_all(parts, axis, split_axis=0, concat_axis=0, tiled=True)  7.55 us
    all_to_all x1, waiting for transfers between devices, summed_on_arrival(): lax.all_to_all(parts, axis, split_axis=0, concat_axis=0, tiled=True)  7.1 us
  transfers between devices with their start and end apart: 18, of which 7 were waited for; matrix products, arithmetic and copies ran while one was open for 15% of the time, Pallas kernels for 0%

commit v1 on v0

v1 whole, which is shorter than its diff:
```python
import jax
import jax.numpy as jnp
from jax import lax
from jax.experimental import pallas as pl
from jax.experimental.pallas import tpu as pltpu
from jax.sharding import PartitionSpec as P

MESH = pl.DeviceIdType.MESH
K = 8
LEV = 16
STEPS = 6
RB = 8
COLS = 384
WIDE = 512
ROWS = 48
FAR = (4, 3, 5, 2, 6, 1, 7)
NEAR = (0, 1, 7, 2, 6, 3, 5, 4)


def kernel(
    inc, adv, dif, dep, obs, err, pen, fst, fwt, out,
    s0, s1, s2, s3, s4, s5, s6, kb, ab, db, force, mis, v0, v1, cv,
    cl, ce, ct, w, pks, pkr, pkm, xt, at, dt, dpt, u0, u1, rs, rr, ps, pr, gr,
    sem_x, sem_a, sem_d, sem_dep, sem_ce,
    a_send, a_recv, ct_send, ct_recv, pk_send, pk_recv, pm_send, pm_recv, pc_send, pc_recv, lc_send, lc_recv,
    h_send, h_recv, w_send, w_recv, r_send, r_recv, p_send, p_recv, g_send, g_recv,
):
    states = (s0, s1, s2, s3, s4, s5, s6)
    tm, lat, lon = lax.axis_index("tm"), lax.axis_index("lat"), lax.axis_index("lon")
    core = lax.rem(lat, 2)
    q = lat // 2
    other = 1 - core
    level = 2 * tm + core
    east, west = lax.rem(lon + 1, 4), lax.rem(lon + 3, 4)
    has_up, has_down = q < 7, q > 0
    lat_up, lat_down = lat < 15, lat > 0

    def remote(src, dst, send, recv, to):
        return pltpu.make_async_remote_copy(
            src_ref=src, dst_ref=dst, send_sem=send, recv_sem=recv, device_id=to, device_id_type=MESH
        )

    def local(src, dst, sem):
        return pltpu.make_async_copy(src, dst, sem)

    stage_x = [local(inc.at[:, r, :], xt.at[r], sem_x) for r in range(RB)]
    stage_a = [local(adv.at[:, r, :], at.at[r], sem_a) for r in range(RB)]
    stage_d = [local(dif.at[:, r, :], dt.at[r], sem_d) for r in range(RB)]
    stage_dep = [local(dep.at[:, :, r, :], dpt.at[r], sem_dep) for r in range(RB)]
    stage_ce = [
        local(src.at[pl.ds(2 * tm, 2)], ce.at[a, :, :, pl.ds(0, COLS)], sem_ce.at[a]) for a, src in enumerate((adv, dif))
    ]
    for c in stage_x:
        c.start()

    barrier = pltpu.get_barrier_semaphore()
    peers = [(lax.rem(tm + d, 8), lat - core + (core if e == 0 else other), lon) for d in range(8) for e in range(2)][1:]
    peers += [(tm, lat, east), (tm, lat, west)]
    peers += [(tm, lax.rem(lat + 2, 16), lon), (tm, lax.rem(lat + 14, 16), lon)]
    peers += [(tm, lax.rem(lat + 15 + 2 * core, 16), lon)]
    for p in peers:
        pl.semaphore_signal(barrier, inc=1, device_id=p, device_id_type=MESH)
    for group in (stage_ce, stage_a, stage_d, stage_dep):
        for c in group:
            c.start()
    pl.semaphore_wait(barrier, len(peers))

    sent_a = []
    for d in FAR + (0,):
        for e in (1, 0):
            if d == 0 and e == 0:
                continue
            to_tm, to_core = lax.rem(tm + d, 8), (core if e == 0 else other)
            sent_a.append(
                remote(
                    inc.at[2 * to_tm + to_core],
                    s0.at[pl.ds(16 + 8 * core, RB), tm, pl.ds(0, COLS)],
                    a_send,
                    a_recv.at[2 * d + e],
                    (to_tm, lat - core + to_core, lon),
                )
            )
    self_a = local(inc.at[level], s0.at[pl.ds(16 + 8 * core, RB), tm, pl.ds(0, COLS)], a_recv.at[0])
    sent_ct = []
    for a, src in enumerate((adv, dif)):
        pair = src.at[pl.ds(2 * tm, 2)]
        sent_ct.append(remote(pair.at[:, :, pl.ds(256, 128)], ct.at[0, a], ct_send.at[a, 0], ct_recv.at[a, 0], (tm, lat, east)))
        sent_ct.append(remote(pair.at[:, :, pl.ds(0, 128)], ct.at[1, a], ct_send.at[a, 1], ct_recv.at[a, 1], (tm, lat, west)))
    for c in sent_a:
        c.start()
    self_a.start()
    for c in sent_ct:
        c.start()

    lane16 = lax.broadcasted_iota(jnp.int32, (LEV, 128), 1)
    lane8 = lax.broadcasted_iota(jnp.int32, (8, 128), 1)

    local(xt, xt, sem_x).wait()
    packed = jnp.zeros((LEV, 128), jnp.float32)
    for r in range(RB):
        edge = jnp.where(lane16 >= 122, xt[r, :, 256:384], xt[r, :, 0:128])
        rolled = pltpu.roll(edge, 12 * r + 6, 1)
        packed = jnp.where((lane16 >= 12 * r) & (lane16 < 12 * r + 12), rolled, packed)
    pks[...] = packed
    sent_pk = [
        remote(pks, pkr.at[0], pk_send.at[0], pk_recv.at[0], (tm, lat, east)),
        remote(pks, pkr.at[1], pk_send.at[1], pk_recv.at[1], (tm, lat, west)),
    ]
    for c in sent_pk:
        c.start()

    sub = lax.broadcasted_iota(jnp.int32, (8, WIDE), 0)
    for s in range(STEPS):
        t = sub * STEPS + s
        total = jnp.where(t == K * STEPS // 2, -1.0, 0.0)
        for j in range(24):
            total = total + jnp.where(t == fst[j], fwt[j], 0.0)
        cv[s] = total

    @pl.when(jnp.logical_not(has_down))
    def _():
        s0[0:16] = jnp.zeros((16, 8, WIDE), jnp.float32)
        cl[:, 0:2] = jnp.zeros((2, 2, 8, WIDE), jnp.float32)
        w[0:2] = jnp.zeros((2, 8, 128), jnp.float32)

    @pl.when(jnp.logical_not(has_up))
    def _():
        s0[32:48] = jnp.zeros((16, 8, WIDE), jnp.float32)
        cl[:, 4:6] = jnp.zeros((2, 2, 8, WIDE), jnp.float32)
        w[4:6] = jnp.zeros((2, 8, 128), jnp.float32)

    for c in sent_ct:
        c.wait_recv()
    for c in stage_ce:
        c.wait()
    for a in range(2):
        for lv in range(2):
            tile = jnp.where(lane8 >= 122, ct[0, a, lv], jnp.where(lane8 < 6, ct[1, a, lv], 0.0))
            ce[a, lv, :, 384:512] = tile
    sent_pc = remote(ce.at[:, other], cl.at[:, 2 + core], pc_send, pc_recv, (tm, lat - core + other, lon))
    sent_pc.start()
    cl[:, 2 + core] = ce[:, core]

    for stage, whole, sem in ((stage_a, at, sem_a), (stage_d, dt, sem_d), (stage_dep, dpt, sem_dep)):
        local(whole, whole, sem).wait()

    def exchanges(n):
        down = remote(rs.at[n, 0], rr.at[n, 0], r_send.at[n, 0], r_recv.at[n, 0], (tm, lax.rem(lat + 15, 16), lon))
        up = remote(rs.at[n, 1], rr.at[n, 1], r_send.at[n, 1], r_recv.at[n, 1], (tm, lax.rem(lat + 1, 16), lon))
        side = remote(ps.at[n], pr.at[n], p_send.at[n], p_recv.at[n], (tm, lat, west))
        return down, up, side

    us = (u0, u1)

    def dep_send(n):
        u = us[n % 2]
        if n == 0:
            for r in range(RB):
                u[r] = dpt[r, STEPS - 1]
        rs[n, 0] = dt[0] * u[0]
        rs[n, 1] = dt[RB - 1] * u[RB - 1]
        packed = jnp.zeros((LEV, 128), jnp.float32)
        for r in range(RB):
            column = at[r, :, 0:128] * u[r, :, 0:128]
            rolled = column if r == 0 else pltpu.roll(column, r, 1)
            packed = jnp.where(lane16 == r, rolled, packed)
        ps[n] = packed
        down, up, side = exchanges(n)
        pl.when(lat_down)(lambda: down.start())
        pl.when(lat_up)(lambda: up.start())
        side.start()

    def dep_step(n):
        u, new = us[n % 2], us[(n + 1) % 2]
        down, up, side = exchanges(n)

        @pl.when(lat_up)
        def _():
            down.wait_recv()

        @pl.when(jnp.logical_not(lat_up))
        def _():
            rr[n, 0] = jnp.zeros((LEV, COLS), jnp.float32)

        @pl.when(lat_down)
        def _():
            up.wait_recv()

        @pl.when(jnp.logical_not(lat_down))
        def _():
            rr[n, 1] = jnp.zeros((LEV, COLS), jnp.float32)

        side.wait_recv()
        arrived = pr[n]
        for r in range(RB):
            v, a, d = u[r], at[r], dt[r]
            p = pltpu.roll(a * v, COLS - 1, 1)
            above = rr[n, 0] if r == RB - 1 else dt[r + 1] * u[r + 1]
            below = rr[n, 1] if r == 0 else dt[r - 1] * u[r - 1]
            fresh = dpt[r, STEPS - 2 - n] + (1.0 - a - 2.0 * d) * v + (above + below)
            new[r, :, 0:256] = fresh[:, 0:256] + p[:, 0:256]
            last = pltpu.roll(arrived, 127 - r, 1)
            new[r, :, 256:384] = fresh[:, 256:384] + jnp.where(lane16 == 127, last, p[:, 256:384])

    dep_send(0)

    for c in sent_pk:
        c.wait_recv()
    pkm[0] = jnp.where(lax.rem(lane16, 12) < 6, pkr[0], pkr[1])
    sent_pm = []
    for d in FAR + (0,):
        for e in (1, 0):
            if d == 0 and e == 0:
                continue
            to_tm, to_core = lax.rem(tm + d, 8), (core if e == 0 else other)
            sent_pm.append(
                remote(
                    pkm.at[:, 2 * to_tm + to_core, :],
                    w.at[pl.ds(2 + core, 1), tm, :],
                    pm_send,
                    pm_recv,
                    (to_tm, lat - core + to_core, lon),
                )
            )
    self_pm = local(pkm.at[:, level, :], w.at[pl.ds(2 + core, 1), tm, :], pm_recv)
    for c in sent_pm:
        c.start()
    self_pm.start()

    sent_pc.wait_recv()
    sent_lc = (
        remote(cl.at[:, pl.ds(2, 2)], cl.at[:, pl.ds(4, 2)], lc_send.at[0], lc_recv.at[0], (tm, lax.rem(lat + 14, 16), lon)),
        remote(cl.at[:, pl.ds(2, 2)], cl.at[:, pl.ds(0, 2)], lc_send.at[1], lc_recv.at[1], (tm, lax.rem(lat + 2, 16), lon)),
    )
    pl.when(has_down)(lambda: sent_lc[0].start())
    pl.when(has_up)(lambda: sent_lc[1].start())

    dep_step(0)
    dep_send(1)

    sides = (
        (has_down, 16, 32, 0, (tm, lax.rem(lat + 14, 16), lon)),
        (has_up, 20, 4, 1, (tm, lax.rem(lat + 2, 16), lon)),
    )
    for d in NEAR:
        k = lax.rem(tm + 8 - d, 8)
        for e in range(2):
            rows = pl.ds(16 + 8 * (core if e == 0 else other), RB)
            block = s0.at[rows, k, pl.ds(0, COLS)]
            local(block, block, a_recv.at[2 * d + e]).wait()
        for there, start, at_row, i, to in sides:
            copy = remote(
                s0.at[pl.ds(start, 12), k, pl.ds(0, COLS)],
                s0.at[pl.ds(at_row, 12), k, pl.ds(0, COLS)],
                h_send.at[i],
                h_recv.at[i],
                to,
            )
            pl.when(there)(lambda copy=copy: copy.start())
    local(w.at[pl.ds(2, 2)], w.at[pl.ds(2, 2)], pm_recv).wait()
    sent_w = (
        remote(w.at[pl.ds(2, 2)], w.at[pl.ds(4, 2)], w_send.at[0], w_recv.at[0], (tm, lax.rem(lat + 14, 16), lon)),
        remote(w.at[pl.ds(2, 2)], w.at[pl.ds(0, 2)], w_send.at[1], w_recv.at[1], (tm, lax.rem(lat + 2, 16), lon)),
    )
    pl.when(has_down)(lambda: sent_w[0].start())
    pl.when(has_up)(lambda: sent_w[1].start())

    dep_step(1)
    dep_send(2)

    pl.when(has_up)(lambda: sent_lc[0].wait_recv())
    pl.when(has_down)(lambda: sent_lc[1].wait_recv())

    def widen(g, _):
        for r in range(RB):
            a = jnp.broadcast_to(cl[0, g, r : r + 1, :], (8, WIDE))
            d = jnp.broadcast_to(cl[1, g, r : r + 1, :], (8, WIDE))
            ab[8 * g + r] = a
            db[8 * g + r] = d
            kb[8 * g + r] = 1.0 - a - 2.0 * d
        return 0

    lax.fori_loop(0, 6, widen, 0)

    dep_step(2)
    dep_send(3)

    for there, rows, i in ((has_up, pl.ds(32, 12), 0), (has_down, pl.ds(4, 12), 1)):
        block = s0.at[rows, :, pl.ds(0, COLS)]

        @pl.when(there)
        def _(block=block, i=i):
            local(block, block, h_recv.at[i]).wait()
            sent_w[i].wait_recv()

    def unpack(g, _):
        mine = w[g]
        for r in range(RB):
            rolled = pltpu.roll(mine, 122 - 12 * r, 1)
            s0[8 * g + r, :, 384:512] = jnp.where((lane8 < 6) | (lane8 >= 122), rolled, 0.0)
        return 0

    lax.fori_loop(0, 6, unpack, 0)

    for s in range(STEPS):
        now, later = states[s], states[s + 1]

        def forward(i, _, now=now, later=later, s=s):
            r = 5 + s + 2 * i
            x = now[pl.ds(r - 1, 4)]
            rows = pl.ds(r, 2)
            centre = x[1:3]
            moved = pltpu.roll(centre, 1, 2)
            later[rows] = kb[rows] * centre + ab[rows] * moved + db[rows] * (x[2:4] + x[0:2])
            return 0

        lax.fori_loop(0, 19 - s, forward, 0, unroll=True)

    weight_obs, weight_err, weight_pen = obs[level], err[level], pen[level]

    def filtered(i, _):
        rows = pl.ds(11 + 2 * i, 2)
        total = cv[0] * s0[rows]
        for s in range(1, STEPS):
            total = total + cv[s] * states[s][rows]
        summed = weight_pen * jnp.sum(total, axis=1, keepdims=True)
        force[rows] = jnp.broadcast_to(summed, (2, 8, WIDE))
        return 0

    lax.fori_loop(0, 13, filtered, 0, unroll=True)

    first = lax.broadcasted_iota(jnp.int32, (2, 8, WIDE), 1) == 0
    final = lax.broadcasted_iota(jnp.int32, (2, 8, WIDE), 1) == 7

    def start(i, _):
        rows = pl.ds(10 + 2 * i, 2)
        m = s0[rows] - jnp.where(first, 0.0, pltpu.roll(s6[rows], 1, 1))
        mis[rows] = jnp.where(first, m, weight_err * m)
        v0[rows] = jnp.where(final, 0.0, -weight_err * pltpu.roll(m, 7, 1))
        return 0

    lax.fori_loop(0, 14, start, 0, unroll=True)

    vs = (v0, v1)
    for n in range(1, STEPS + 1):
        s = STEPS - n
        now, later = vs[(n + 1) % 2], vs[n % 2]

        def backward(i, _, now=now, later=later, s=s, n=n):
            r = 10 + n + 2 * i
            rows = pl.ds(r, 2)
            v = now[pl.ds(r - 1, 4)]
            spread = db[pl.ds(r - 1, 4)] * v
            centre = v[1:3]
            carried = pltpu.roll(ab[rows] * centre, WIDE - 1, 2)
            forcing = weight_obs * states[s][rows] + cv[s] * force[rows]
            fresh = forcing + (kb[rows] * centre + carried + (spread[2:4] + spread[0:2]))
            if s == 0:
                fresh = fresh + mis[rows]
            later[rows] = fresh
            return 0

        lax.fori_loop(0, 14 - n, backward, 0, unroll=True)
    result = vs[STEPS % 2]

    sent_g = []
    for d in FAR + (0,):
        for e in (1, 0):
            if d == 0 and e == 0:
                continue
            to_tm, to_core = lax.rem(tm + d, 8), (core if e == 0 else other)
            sent_g.append(
                remote(
                    result.at[pl.ds(16 + 8 * to_core, RB), to_tm, pl.ds(0, COLS)],
                    gr.at[:, level, :],
                    g_send,
                    g_recv,
                    (to_tm, lat - core + to_core, lon),
                )
            )
    for c in sent_g:
        c.start()
    self_g = local(result.at[pl.ds(16 + 8 * core, RB), tm, pl.ds(0, COLS)], gr.at[:, level, :], g_recv)
    self_g.start()

    dep_step(3)
    dep_send(4)
    level16 = lax.broadcasted_iota(jnp.int32, (LEV, COLS), 0)
    obs_all = jnp.zeros((LEV, COLS), jnp.float32)
    for lv in range(LEV):
        obs_all = jnp.where(level16 == lv, obs[lv], obs_all)
    dep_step(4)

    fifteen = s1.at[pl.ds(0, 15), :, pl.ds(0, COLS)]
    local(fifteen, fifteen, a_send).wait()
    for c in sent_ct + sent_pk + [sent_pc]:
        c.wait_send()

    for c in sent_pm:
        c.wait_send()
    for i, there in enumerate((has_down, has_up)):
        block = s1.at[pl.ds(4, 12), :, pl.ds(0, COLS)]

        @pl.when(there)
        def _(i=i, block=block):
            sent_lc[i].wait_send()
            sent_w[i].wait_send()
            local(block, block, h_send.at[i]).wait()

    for n in range(STEPS - 1):
        down, up, side = exchanges(n)
        pl.when(lat_down)(lambda down=down: down.wait_send())
        pl.when(lat_up)(lambda up=up: up.wait_send())
        side.wait_send()

    local(gr, gr, g_recv).wait()
    for r in range(RB):
        out[r] = gr[r] - obs_all * us[(STEPS - 1) % 2][r]
    local(fifteen, fifteen, g_send).wait()


def body(increments, advection, diffusion, departures, obs, err, pen, steps, weights):
    f32 = jnp.float32
    big = pltpu.VMEM((ROWS, 8, WIDE), f32)
    block = pltpu.VMEM((RB, LEV, COLS), f32)
    dma = pltpu.SemaphoreType.DMA
    scratch = [big] * 14 + [pltpu.VMEM((STEPS, 8, WIDE), f32)]
    scratch += [
        pltpu.VMEM((2, 6, 8, WIDE), f32),
        pltpu.VMEM((2, 2, 8, WIDE), f32),
        pltpu.VMEM((2, 2, 2, 8, 128), f32),
        pltpu.VMEM((6, 8, 128), f32),
        pltpu.VMEM((LEV, 128), f32),
        pltpu.VMEM((2, LEV, 128), f32),
        pltpu.VMEM((1, LEV, 128), f32),
        block,
        block,
        block,
        pltpu.VMEM((RB, STEPS, LEV, COLS), f32),
        block,
        block,
        pltpu.VMEM((STEPS - 1, 2, LEV, COLS), f32),
        pltpu.VMEM((STEPS - 1, 2, LEV, COLS), f32),
        pltpu.VMEM((STEPS - 1, LEV, 128), f32),
        pltpu.VMEM((STEPS - 1, LEV, 128), f32),
        block,
    ]
    scratch += [dma, dma, dma, dma, dma((2,))]
    scratch += [dma, dma((16,)), dma((2, 2)), dma((2, 2)), dma((2,)), dma((2,)), dma, dma, dma, dma, dma((2,)), dma((2,))]
    scratch += [dma((2,)), dma((2,)), dma((2,)), dma((2,)), dma((5, 2)), dma((5, 2)), dma((5,)), dma((5,)), dma, dma]
    any_space = pl.BlockSpec(memory_space=pl.ANY)
    smem = pl.BlockSpec(memory_space=pltpu.SMEM)
    gradient = pl.pallas_call(
        kernel,
        out_shape=jax.ShapeDtypeStruct((RB, LEV, COLS), f32),
        in_specs=[any_space] * 4 + [smem] * 5,
        out_specs=pl.BlockSpec(memory_space=pltpu.VMEM),
        scratch_shapes=scratch,
        compiler_params=pltpu.CompilerParams(
            collective_id=0, has_side_effects=True, vmem_limit_bytes=56 * 1024 * 1024
        ),
        name="gradient",
    )(increments[0], advection, diffusion, departures[0], obs, err, pen, steps, weights)
    return jnp.transpose(gradient, (1, 0, 2))[None]


def solution(mesh):
    return jax.shard_map(
        body,
        mesh=mesh,
        in_specs=(
            P("tm", None, "lat", "lon"),
            P(None, "lat", "lon"),
            P(None, "lat", "lon"),
            P("tm", None, None, "lat", "lon"),
            P(),
            P(),
            P(),
            P(),
            P(),
        ),
        out_specs=P("tm", None, "lat", "lon"),
        check_vma=False,
    )
```

time: 185 us -> 45.9 us (0.25)
  the two profiles are of different devices: /device:TPU:10 before, /device:TPU:1 now
where the time goes in v1:
time: 45.9 us; the launch traced here: 45.7 us
  Pallas kernels  44.1 us (96%)
  local copies, waits for them, and re-layouts  1.67 us (4%)
    pallas_call x1, Pallas kernels, body(): pl.pallas_call(kernel, out_shape=jax.ShapeDtypeStruct((RB, LEV, COLS), f3...  44.1 us
    broadcast_in_dim x1, local copies, waits for them, and re-layouts, body(): return jnp.transpose(gradient, (1, 0, 2))[None]  1.67 us

profile of v1, /device:TPU:1, one launch (start us, length us, event | category | flops | bytes accessed | tf_op | source)
XLA Modules:
  0.0 45.7 jit_solution(952020916978927391)
XLA Ops:
  0.0 44.1 %gradient.1 = f32[8,16,384]{2,1,0:T(8,128)} custom-call(f32[16,8,384]{2,1,0:T(8,128)} %bitcast.7, f32[16,8,384]{2,1,0:T(8,128)} %adv.1, f32[16,8,384]{2,1,0:T(8,128)} %dif.1, f32[6,16,8,384]{3,2,1,0:T(8,128)} %bitcast.5, f32[16]{0:T(128)} %obs.1, f32[16]{0:T(128)} %err.1, f32[16]{0:T(128)} %pen.1, s32[24]{0:T(128)} %fst.1, f32[24]{0:T(128)} %fwt.1), custom_call_target="tpu_custom_call" | custom-call | tf_op jit(solution)/shard_map/gradient/pallas_call | solution.py:453
  44.1 1.7 %copy.10 = f32[1,16,8,384]{3,2,1,0:T(8,128)} copy(f32[1,16,8,384]{3,1,2,0:T(8,128)} %bitcast.6) | data formatting | bytes 393216 | tf_op jit(solution)/shard_map/broadcast_in_dim | solution.py:464

commit v2 on v1

v2 whole, which is shorter than its diff:
```python
import jax
import jax.numpy as jnp
from jax import lax
from jax.experimental import pallas as pl
from jax.experimental.pallas import tpu as pltpu
from jax.sharding import PartitionSpec as P

MESH = pl.DeviceIdType.MESH
K = 8
LEV = 16
STEPS = 6
RB = 8
COLS = 384
WIDE = 512
ROWS = 48
FAR = (4, 3, 5, 2, 6, 1, 7)
NEAR = (0, 1, 7, 2, 6, 3, 5, 4)


def kernel(
    inc, adv, dif, dep, obs_h, err_h, pen_h, fst_h, fwt_h, out, obs, err, pen, fst, fwt,
    s0, s1, s2, s3, s4, s5, s6, kb, ab, db, force, mis, v0, v1, cv,
    cl, ae, w, pks, pkr, pkm, lp, xt, dpt, u0, u1, lr, ps, pr, gr,
    sem_x, sem_ae, sem_dep, sem_small, sem_out,
    a_send, a_recv, pk_send, pk_recv, pm_send, pm_recv, pc_send, pc_recv, lc_send, lc_recv,
    h_send, h_recv, w_send, w_recv, e_send, e_recv, lp_send, lp_recv, r_send, r_recv, p_send, p_recv, g_send, g_recv,
):
    states = (s0, s1, s2, s3, s4, s5, s6)
    tm, lat, lon = lax.axis_index("tm"), lax.axis_index("lat"), lax.axis_index("lon")
    core = lax.rem(lat, 2)
    pair = lax.rem(lat // 2, 2)
    base = lat - lax.rem(lat, 4)
    level = 2 * tm + pair
    east, west = lax.rem(lon + 1, 4), lax.rem(lon + 3, 4)
    has_up, has_down = (base < 12) | (core == 0), (base > 0) | (core == 1)
    owner_up = (tm, lax.rem(lat + 1 + 2 * core, 16), lon)
    owner_down = (tm, lax.rem(lat + 13 + 2 * core, 16), lon)
    lat_up, lat_down = lat < 15, lat > 0

    def remote(src, dst, send, recv, to):
        return pltpu.make_async_remote_copy(
            src_ref=src, dst_ref=dst, send_sem=send, recv_sem=recv, device_id=to, device_id_type=MESH
        )

    def local(src, dst, sem):
        return pltpu.make_async_copy(src, dst, sem)

    stage_x = [local(inc.at[:, r, :], xt.at[r], sem_x) for r in range(RB)]
    stage_ae = [
        local(src.at[:, r, :], ae.at[a, 8 + r, :, pl.ds(0, COLS)], sem_ae)
        for a, src in enumerate((adv, dif))
        for r in range(RB)
    ]
    stage_dep = [local(dep.at[:, :, r, :], dpt.at[r], sem_dep) for r in range(RB)]
    small = [
        local(src, dst, sem_small.at[i])
        for i, (src, dst) in enumerate(((obs_h, obs), (err_h, err), (pen_h, pen), (fst_h, fst), (fwt_h, fwt)))
    ]
    for c in stage_x + stage_ae:
        c.start()

    barrier = pltpu.get_barrier_semaphore()
    at_end = (lax.rem(lat, 4) == 0) | (lax.rem(lat, 4) == 3)
    peers = [(lax.rem(tm + d, 8), base + lax.rem(lat + i, 4), lon) for d in FAR + (0,) for i in range(4)]
    del peers[28]
    peers += [(tm, lat, east), (tm, lat, west), (tm, lax.rem(lat + 13 + 6 * core, 16), lon)]
    for p in peers:
        pl.semaphore_signal(barrier, inc=1, device_id=p, device_id_type=MESH)

    @pl.when(at_end)
    def _():
        end = lax.rem(lat + 15 + 2 * core, 16)
        pl.semaphore_signal(barrier, inc=1, device_id=(tm, end, lon), device_id_type=MESH)

    for c in stage_dep + small:
        c.start()

    u0[...] = jnp.zeros(u0.shape, jnp.float32)
    u1[...] = jnp.zeros(u1.shape, jnp.float32)

    pl.semaphore_wait(barrier, len(peers) + at_end.astype(jnp.int32))

    def start_to(to, myself, src, dst, send, recv):
        copy = remote(src, dst, send, recv, to)
        if myself is None:
            copy.start()
            return
        pl.when(jnp.logical_not(myself))(lambda: copy.start())
        pl.when(myself)(lambda: local(src, dst, recv).start())

    diagonal = core == pair

    for d in FAR + (0,):
        to_tm = lax.rem(tm + d, 8)
        for e in range(2):
            p = lax.rem(pair + 1 + e, 2)
            start_to(
                (to_tm, base + 2 * p + pair, lon),
                diagonal if d == 0 and e == 1 else None,
                inc.at[2 * to_tm + p],
                s0.at[pl.ds(16 + 8 * core, RB), tm, pl.ds(0, COLS)],
                a_send,
                a_recv.at[2 * d + core],
            )
    lane16 = lax.broadcasted_iota(jnp.int32, (LEV, 128), 1)
    lane8 = lax.broadcasted_iota(jnp.int32, (8, 128), 1)

    local(xt, xt, sem_x).wait()
    own = ae.at[:, pl.ds(8, RB), :, pl.ds(0, COLS)]
    local(own, own, sem_ae).wait()
    for f in range(3):
        packed = jnp.zeros((LEV, 128), jnp.float32)
        for r in range(RB):
            field = xt.at[r] if f == 0 else ae.at[f - 1, 8 + r]
            edge = jnp.where(lane16 >= 122, field[:, 256:384], field[:, 0:128])
            rolled = pltpu.roll(edge, 12 * r + 6, 1)
            packed = jnp.where((lane16 >= 12 * r) & (lane16 < 12 * r + 12), rolled, packed)
        pks[f] = packed
    sent_pk = [
        remote(pks, pkr.at[0], pk_send.at[0], pk_recv.at[0], (tm, lat, east)),
        remote(pks, pkr.at[1], pk_send.at[1], pk_recv.at[1], (tm, lat, west)),
    ]
    for c in sent_pk:
        c.start()

    band_up, band_down = (tm, lax.rem(lat + 1, 16), lon), (tm, lax.rem(lat + 15, 16), lon)

    def rows_of(first):
        return ae.at[:, pl.ds(first, 5), :, pl.ds(0, COLS)]

    sent_e = (
        remote(rows_of(8), rows_of(16), e_send.at[0], e_recv.at[0], band_down),
        remote(rows_of(11), rows_of(3), e_send.at[1], e_recv.at[1], band_up),
    )
    pl.when(lat_down)(lambda: sent_e[0].start())
    pl.when(lat_up)(lambda: sent_e[1].start())

    for c in small:
        c.wait()
    sub = lax.broadcasted_iota(jnp.int32, (8, WIDE), 0)
    for s in range(STEPS):
        t = sub * STEPS + s
        total = jnp.where(t == K * STEPS // 2, -1.0, 0.0)
        for j in range(24):
            total = total + jnp.where(t == fst[j], fwt[j], 0.0)
        cv[s] = total

    @pl.when(jnp.logical_not(has_down))
    def _():
        s0[0:16] = jnp.zeros((16, 8, WIDE), jnp.float32)
        cl[:, 0:2] = jnp.zeros((2, 2, 8, WIDE), jnp.float32)
        w[0:2] = jnp.zeros((2, 8, 128), jnp.float32)

    @pl.when(jnp.logical_not(has_up))
    def _():
        s0[32:48] = jnp.zeros((16, 8, WIDE), jnp.float32)
        cl[:, 4:6] = jnp.zeros((2, 2, 8, WIDE), jnp.float32)
        w[4:6] = jnp.zeros((2, 8, 128), jnp.float32)

    @pl.when(jnp.logical_not(lat_down))
    def _():
        ae[:, 3:8] = jnp.zeros((2, 5, LEV, WIDE), jnp.float32)
        lr[0] = jnp.zeros((5, LEV, COLS), jnp.float32)

    @pl.when(jnp.logical_not(lat_up))
    def _():
        ae[:, 16:21] = jnp.zeros((2, 5, LEV, WIDE), jnp.float32)
        lr[1] = jnp.zeros((5, LEV, COLS), jnp.float32)

    local(dpt, dpt, sem_dep).wait()
    us = (u0, u1)
    for r in range(RB):
        u0[8 + r, :, 0:COLS] = dpt[r, STEPS - 1]

    def dep_step(n):
        u, new = us[(n + 1) % 2], us[n % 2]

        def moved(r):
            v, a, d = u[r], ae[0, r], ae[1, r]
            p = pltpu.roll(a * v, WIDE - 1, 1)
            return (1.0 - a - 2.0 * d) * v + p + (ae[1, r + 1] * u[r + 1] + ae[1, r - 1] * u[r - 1])

        def outer(r, _):
            new[r] = moved(r)
            return 0

        def inner(r, _):
            fresh = moved(r)
            new[r, :, 0:COLS] = fresh[:, 0:COLS] + dpt[r - 8, STEPS - 1 - n]
            new[r, :, COLS:WIDE] = fresh[:, COLS:WIDE]
            return 0

        lax.fori_loop(8 - n, 8, outer, 0, unroll=True)
        lax.fori_loop(8, 16, inner, 0, unroll=True)
        lax.fori_loop(16, 16 + n, outer, 0, unroll=True)

    sides = ((has_down, 16, 32, 0, owner_down), (has_up, 20, 4, 1, owner_up))

    def pass_on(d):
        k = lax.rem(tm + 8 - d, 8)
        for e in range(2):
            block = s0.at[pl.ds(16 + 8 * e, RB), k, pl.ds(0, COLS)]
            local(block, block, a_recv.at[2 * d + e]).wait()
        for there, start, at_row, i, to in sides:
            copy = remote(
                s0.at[pl.ds(start, 12), k, pl.ds(0, COLS)],
                s0.at[pl.ds(at_row, 12), k, pl.ds(0, COLS)],
                h_send.at[i],
                h_recv.at[i],
                to,
            )
            pl.when(there)(lambda copy=copy: copy.start())

    for d in NEAR[:3]:
        pass_on(d)

    for c in sent_pk:
        c.wait_recv()
    for f in range(3):
        pkm[f] = jnp.where(lax.rem(lane16, 12) < 6, pkr[0, f], pkr[1, f])
    for d in FAR + (0,):
        to_tm = lax.rem(tm + d, 8)
        for e in range(2):
            p = lax.rem(pair + 1 + e, 2)
            start_to(
                (to_tm, base + 2 * p + pair, lon),
                diagonal if d == 0 and e == 1 else None,
                pkm.at[pl.ds(0, 1), 2 * to_tm + p, :],
                w.at[pl.ds(2 + core, 1), tm, :],
                pm_send,
                pm_recv,
            )

    halo_lanes = (lane16 < 6) | (lane16 >= 122)

    def tile_of(packed, r):
        return jnp.where(halo_lanes, pltpu.roll(packed, 122 - 12 * r, 1), 0.0)

    for a in range(2):
        for r in range(RB):
            ae[a, 8 + r, :, COLS:WIDE] = tile_of(pkm[1 + a], r)
    for e in range(2):
        p = lax.rem(pair + 1 + e, 2)
        start_to(
            (tm, base + 2 * p + pair, lon),
            diagonal if e == 1 else None,
            ae.at[:, pl.ds(8, RB), 2 * tm + p, :],
            cl.at[:, 2 + core],
            pc_send,
            pc_recv,
        )
    packed_coefs = pkm.at[pl.ds(1, 2)]
    sent_lp = (
        remote(packed_coefs, lp.at[1], lp_send.at[0], lp_recv.at[0], band_down),
        remote(packed_coefs, lp.at[0], lp_send.at[1], lp_recv.at[1], band_up),
    )
    pl.when(lat_down)(lambda: sent_lp[0].start())
    pl.when(lat_up)(lambda: sent_lp[1].start())

    for d in NEAR[3:5]:
        pass_on(d)

    mine = cl.at[:, pl.ds(2, 2)]
    local(mine, mine, pc_recv).wait()
    sent_lc = (
        remote(mine, cl.at[:, pl.ds(4, 2)], lc_send.at[0], lc_recv.at[0], owner_down),
        remote(mine, cl.at[:, pl.ds(0, 2)], lc_send.at[1], lc_recv.at[1], owner_up),
    )
    pl.when(has_down)(lambda: sent_lc[0].start())
    pl.when(has_up)(lambda: sent_lc[1].start())

    @pl.when(lat_up)
    def _():
        sent_e[0].wait_recv()
        sent_lp[0].wait_recv()
        for a in range(2):
            for r in range(5):
                ae[a, 16 + r, :, COLS:WIDE] = tile_of(lp[1, a], r)

    @pl.when(lat_down)
    def _():
        sent_e[1].wait_recv()
        sent_lp[1].wait_recv()
        for a in range(2):
            for r in range(5):
                ae[a, 3 + r, :, COLS:WIDE] = tile_of(lp[0, a], 3 + r)

    dep_step(1)
    pass_on(NEAR[5])
    dep_step(2)
    pass_on(NEAR[6])
    pass_on(NEAR[7])
    local(w.at[pl.ds(2, 2)], w.at[pl.ds(2, 2)], pm_recv).wait()
    sent_w = (
        remote(w.at[pl.ds(2, 2)], w.at[pl.ds(4, 2)], w_send.at[0], w_recv.at[0], owner_down),
        remote(w.at[pl.ds(2, 2)], w.at[pl.ds(0, 2)], w_send.at[1], w_recv.at[1], owner_up),
    )
    pl.when(has_down)(lambda: sent_w[0].start())
    pl.when(has_up)(lambda: sent_w[1].start())
    dep_step(3)
    dep_step(4)
    dep_step(5)
    us_end = us[1]
    packed = jnp.zeros((LEV, 128), jnp.float32)
    for i in range(18):
        rolled = pltpu.roll(us_end[3 + i, :, COLS:WIDE], 5 * i + 5, 1)
        packed = jnp.where((lane16 >= 5 * i) & (lane16 < 5 * i + 5), rolled, packed)
    ps[...] = packed
    sent_p = remote(ps, pr, p_send, p_recv, (tm, lat, west))
    sent_p.start()

    pl.when(has_up)(lambda: sent_lc[0].wait_recv())
    pl.when(has_down)(lambda: sent_lc[1].wait_recv())

    def widen(g, _):
        for r in range(RB):
            a = jnp.broadcast_to(cl[0, g, r : r + 1, :], (8, WIDE))
            d = jnp.broadcast_to(cl[1, g, r : r + 1, :], (8, WIDE))
            ab[8 * g + r] = a
            db[8 * g + r] = d
            kb[8 * g + r] = 1.0 - a - 2.0 * d
        return 0

    lax.fori_loop(0, 6, widen, 0)

    for there, rows, i in ((has_up, pl.ds(32, 12), 0), (has_down, pl.ds(4, 12), 1)):
        block = s0.at[rows, :, pl.ds(0, COLS)]

        @pl.when(there)
        def _(block=block, i=i):
            local(block, block, h_recv.at[i]).wait()
            sent_w[i].wait_recv()

    def unpack(g, _):
        mine = w[g]
        for r in range(RB):
            rolled = pltpu.roll(mine, 122 - 12 * r, 1)
            s0[8 * g + r, :, 384:512] = jnp.where((lane8 < 6) | (lane8 >= 122), rolled, 0.0)
        return 0

    lax.fori_loop(0, 6, unpack, 0)

    for s in range(STEPS):
        now, later = states[s], states[s + 1]

        def forward(i, _, now=now, later=later, s=s):
            r = 5 + s + 2 * i
            x = now[pl.ds(r - 1, 4)]
            rows = pl.ds(r, 2)
            centre = x[1:3]
            moved = pltpu.roll(centre, 1, 2)
            later[rows] = kb[rows] * centre + ab[rows] * moved + db[rows] * (x[2:4] + x[0:2])
            return 0

        lax.fori_loop(0, 19 - s, forward, 0, unroll=True)

    sent_p.wait_recv()
    for i in range(18):
        rolled = pltpu.roll(pr[...], (123 - 5 * i) % 128, 1)
        us_end[3 + i, :, 256:384] = us_end[3 + i, :, 256:384] + jnp.where(lane16 >= 123, rolled, 0.0)
    sent_r = (
        remote(us_end.at[pl.ds(3, 5), :, pl.ds(0, COLS)], lr.at[1], r_send.at[0], r_recv.at[0], band_down),
        remote(us_end.at[pl.ds(16, 5), :, pl.ds(0, COLS)], lr.at[0], r_send.at[1], r_recv.at[1], band_up),
    )
    pl.when(lat_down)(lambda: sent_r[0].start())
    pl.when(lat_up)(lambda: sent_r[1].start())

    weight_obs, weight_err, weight_pen = obs[level], err[level], pen[level]

    def filtered(i, _):
        rows = pl.ds(11 + 2 * i, 2)
        total = cv[0] * s0[rows]
        for s in range(1, STEPS):
            total = total + cv[s] * states[s][rows]
        summed = weight_pen * jnp.sum(total, axis=1, keepdims=True)
        force[rows] = jnp.broadcast_to(summed, (2, 8, WIDE))
        return 0

    lax.fori_loop(0, 13, filtered, 0, unroll=True)

    first = lax.broadcasted_iota(jnp.int32, (2, 8, WIDE), 1) == 0
    final = lax.broadcasted_iota(jnp.int32, (2, 8, WIDE), 1) == 7

    def start(i, _):
        rows = pl.ds(10 + 2 * i, 2)
        m = s0[rows] - jnp.where(first, 0.0, pltpu.roll(s6[rows], 1, 1))
        mis[rows] = jnp.where(first, m, weight_err * m)
        v0[rows] = jnp.where(final, 0.0, -weight_err * pltpu.roll(m, 7, 1))
        return 0

    lax.fori_loop(0, 14, start, 0, unroll=True)

    vs = (v0, v1)
    for n in range(1, STEPS + 1):
        s = STEPS - n
        now, later = vs[(n + 1) % 2], vs[n % 2]

        def backward(i, _, now=now, later=later, s=s, n=n):
            r = 10 + n + 2 * i
            rows = pl.ds(r, 2)
            v = now[pl.ds(r - 1, 4)]
            spread = db[pl.ds(r - 1, 4)] * v
            centre = v[1:3]
            carried = pltpu.roll(ab[rows] * centre, WIDE - 1, 2)
            forcing = weight_obs * states[s][rows] + cv[s] * force[rows]
            fresh = forcing + (kb[rows] * centre + carried + (spread[2:4] + spread[0:2]))
            if s == 0:
                fresh = fresh + mis[rows]
            later[rows] = fresh
            return 0

        if s > 0:
            lax.fori_loop(0, 14 - n, backward, 0, unroll=True)
            continue
        for half in range(2):
            lax.fori_loop(4 * half, 4 * half + 4, backward, 0, unroll=True)
            for d in FAR + (0,):
                to_tm = lax.rem(tm + d, 8)
                to = base + 2 * core + half
                start_to(
                    (to_tm, to, lon),
                    to == lat if d == 0 else None,
                    later.at[pl.ds(16 + 8 * half, RB), to_tm, pl.ds(0, COLS)],
                    gr.at[:, level, :],
                    g_send,
                    g_recv,
                )

    level16 = lax.broadcasted_iota(jnp.int32, (LEV, COLS), 0)
    obs_all = jnp.zeros((LEV, COLS), jnp.float32)
    for lv in range(LEV):
        obs_all = jnp.where(level16 == lv, obs[lv], obs_all)
    pl.when(lat_up)(lambda: sent_r[0].wait_recv())
    pl.when(lat_down)(lambda: sent_r[1].wait_recv())
    for r in range(RB):
        total = us_end[8 + r, :, 0:COLS]
        if r < 5:
            total = total + lr[0, r]
        if r >= 3:
            total = total + lr[1, r - 3]
        xt[r] = obs_all * total

    def drain(whole, fewer, sem):
        pl.when(diagonal)(lambda: local(fewer, fewer, sem).wait())
        pl.when(jnp.logical_not(diagonal))(lambda: local(whole, whole, sem).wait())

    sixteen, fifteen = (s1.at[pl.ds(0, n), :, pl.ds(0, COLS)] for n in (16, 15))
    drain(sixteen, fifteen, a_send)
    drain(cl.at[:, pl.ds(0, 2)], cl.at[:, 0], pc_send)
    drain(pkm.at[0], pkm.at[0, pl.ds(0, 15)], pm_send)
    for c in sent_pk + [sent_p]:
        c.wait_send()
    for i, there in enumerate((has_down, has_up)):
        block = s1.at[pl.ds(4, 12), :, pl.ds(0, COLS)]

        @pl.when(there)
        def _(i=i, block=block):
            sent_lc[i].wait_send()
            sent_w[i].wait_send()
            local(block, block, h_send.at[i]).wait()

    for i, there in enumerate((lat_down, lat_up)):

        @pl.when(there)
        def _(i=i):
            for c in (sent_e[i], sent_lp[i], sent_r[i]):
                c.wait_send()

    local(gr, gr, g_recv).wait()
    for r in range(RB):
        xt[r] = gr[r] - xt[r]
        local(xt.at[r], out.at[:, r, :], sem_out).start()
    drain(sixteen, fifteen, g_send)
    local(xt, xt, sem_out).wait()


def body(increments, advection, diffusion, departures, obs, err, pen, steps, weights):
    f32 = jnp.float32
    big = pltpu.VMEM((ROWS, 8, WIDE), f32)
    block = pltpu.VMEM((RB, LEV, COLS), f32)
    dma = pltpu.SemaphoreType.DMA
    scratch = [pltpu.SMEM((LEV,), f32)] * 3 + [pltpu.SMEM((24,), jnp.int32), pltpu.SMEM((24,), f32)]
    scratch += [big] * 14 + [pltpu.VMEM((STEPS, 8, WIDE), f32)]
    scratch += [
        pltpu.VMEM((2, 6, 8, WIDE), f32),
        pltpu.VMEM((2, 24, LEV, WIDE), f32),
        pltpu.VMEM((6, 8, 128), f32),
        pltpu.VMEM((3, LEV, 128), f32),
        pltpu.VMEM((2, 3, LEV, 128), f32),
        pltpu.VMEM((3, LEV, 128), f32),
        pltpu.VMEM((2, 2, LEV, 128), f32),
        block,
        pltpu.VMEM((RB, STEPS, LEV, COLS), f32),
        pltpu.VMEM((24, LEV, WIDE), f32),
        pltpu.VMEM((24, LEV, WIDE), f32),
        pltpu.VMEM((2, 5, LEV, COLS), f32),
        pltpu.VMEM((LEV, 128), f32),
        pltpu.VMEM((LEV, 128), f32),
        block,
    ]
    scratch += [dma, dma, dma, dma((5,)), dma]
    scratch += [dma, dma((16,)), dma((2,)), dma((2,)), dma, dma, dma, dma, dma((2,)), dma((2,))]
    scratch += [dma((2,))] * 8 + [dma((2,)), dma((2,)), dma, dma, dma, dma]
    any_space = pl.BlockSpec(memory_space=pl.ANY)
    gradient = pl.pallas_call(
        kernel,
        out_shape=jax.ShapeDtypeStruct((LEV, RB, COLS), f32),
        in_specs=[any_space] * 9,
        out_specs=any_space,
        scratch_shapes=scratch,
        compiler_params=pltpu.CompilerParams(
            collective_id=0, has_side_effects=True, vmem_limit_bytes=56 * 1024 * 1024
        ),
        name="gradient",
    )(increments[0], advection, diffusion, departures[0], obs, err, pen, steps, weights)
    return gradient[None]


def solution(mesh):
    return jax.shard_map(
        body,
        mesh=mesh,
        in_specs=(
            P("tm", None, "lat", "lon"),
            P(None, "lat", "lon"),
            P(None, "lat", "lon"),
            P("tm", None, None, "lat", "lon"),
            P(),
            P(),
            P(),
            P(),
            P(),
        ),
        out_specs=P("tm", None, "lat", "lon"),
        check_vma=False,
    )
```

time: 45.9 us -> 40.6 us (0.88); the launches traced: 45.7 us -> 39.9 us
  Pallas kernels: 44.1 us -> 38.3 us
    pallas_call x1, Pallas kernels: 44.1 us -> 38.3 us  [body(): pl.pallas_call(kernel, out_shape=jax.ShapeDtypeStruct((LEV, RB, COLS), f3...]
    broadcast_in_dim x1 -> x0, local copies, waits for them, and re-layouts: 1.67 us -> none  [body(): return jnp.transpose(gradient, (1, 0, 2))[None]]
    unnamed x0 -> x1, local copies, waits for them, and re-layouts: none -> 1.62 us
where the time goes in v2:
time: 40.6 us; the launch traced here: 39.9 us
  Pallas kernels  38.3 us (94%)
  local copies, waits for them, and re-layouts  1.62 us (4%)
    pallas_call x1, Pallas kernels, body(): pl.pallas_call(kernel, out_shape=jax.ShapeDtypeStruct((LEV, RB, COLS), f3...  38.3 us
    unnamed x1, local copies, waits for them, and re-layouts  1.62 us

profile of v2, /device:TPU:1, one launch (start us, length us, event | category | flops | bytes accessed | tf_op | source)
XLA Modules:
  0.0 39.9 jit_solution(1077654721532567724)
XLA Ops:
  0.0 38.3 %gradient.1 = f32[16,8,384]{2,1,0:T(8,128)} custom-call(f32[16,8,384]{2,1,0:T(8,128)} %bitcast.5, f32[16,8,384]{2,1,0:T(8,128)} %adv.1, f32[16,8,384]{2,1,0:T(8,128)} %dif.1, f32[6,16,8,384]{3,2,1,0:T(8,128)} %bitcast.3, f32[16]{0:T(128)} %obs_h.1, f32[16]{0:T(128)} %err_h.1, f32[16]{0:T(128)} %pen_h.1, s32[24]{0:T(128)} %fst_h.1, f32[24]{0:T(128)} %fwt_h.1), custom_call_target="tpu_custom_call" | custom-call | tf_op jit(solution)/shard_map/gradient/pallas_call | solution.py:505
  38.3 1.6 %copy.11 = f32[1,16,8,384]{3,2,1,0:T(8,128)} copy(f32[1,16,8,384]{3,2,1,0:T(8,128)} %bitcast.4) | data formatting | bytes 393216

commit v3 on v2

v3 whole, which is shorter than its diff:
```python
import jax
import jax.numpy as jnp
from jax import lax
from jax.experimental import pallas as pl
from jax.experimental.pallas import tpu as pltpu
from jax.sharding import PartitionSpec as P

MESH = pl.DeviceIdType.MESH
K = 8
LEV = 16
STEPS = 6
RB = 8
COLS = 384
WIDE = 512
ROWS = 48
FAR = (4, 3, 5, 2, 6, 1, 7)
VMEM_KIB = 64 * 1024 - 560
OUT = pltpu.VMEM
NEAR = (0, 1, 7, 2, 6, 3, 5, 4)


def kernel(
    inc, adv, dif, dep, obs_h, err_h, pen_h, fst_h, fwt_h, gr, moved_back, obs, err, pen, fst, fwt,
    s0, s1, s2, s3, s4, s5, s6, kb, ab, db, force, mis, v0, v1, cv,
    cl, cw, ae, ws, pks, lp, xt, dpt, u0, u1, lr, ps, pr,
    answer, sem_x, sem_ae, sem_dep, sem_small,
    a_send, a_recv, ws_send, ws_recv, cl_send, cl_recv, cw_send, cw_recv,
    h_send, h_recv, e_send, e_recv, lp_send, lp_recv, r_send, r_recv, p_send, p_recv, g_send, g_recv,
):
    states = (s0, s1, s2, s3, s4, s5, s6)
    tm, lat, lon = lax.axis_index("tm"), lax.axis_index("lat"), lax.axis_index("lon")
    core = lax.rem(lat, 2)
    pair = lax.rem(lat // 2, 2)
    base = lat - lax.rem(lat, 4)
    level = 2 * tm + pair
    has_up, has_down = (base < 12) | (core == 0), (base > 0) | (core == 1)
    chip_up, chip_down = (base < 12) | (pair == 0), (base > 0) | (pair == 1)
    owner_up = (tm, lax.rem(lat + 1 + 2 * core, 16), lon)
    owner_down = (tm, lax.rem(lat + 13 + 2 * core, 16), lon)
    lat_up, lat_down = lat < 15, lat > 0
    above, below = lax.rem(lat + 1, 16), lax.rem(lat + 15, 16)
    band_up, band_down = (tm, above, lon), (tm, below, lon)

    def remote(src, dst, send, recv, to):
        return pltpu.make_async_remote_copy(
            src_ref=src, dst_ref=dst, send_sem=send, recv_sem=recv, device_id=to, device_id_type=MESH
        )

    def local(src, dst, sem):
        return pltpu.make_async_copy(src, dst, sem)

    def not_(flag):
        return jnp.logical_not(flag)

    stage_x = [local(inc.at[:, r, :], xt.at[r], sem_x) for r in range(RB)]
    stage_ae = [
        local(src.at[:, r, :], ae.at[a, 8 + r, :, pl.ds(0, COLS)], sem_ae)
        for a, src in enumerate((adv, dif))
        for r in range(RB)
    ]
    stage_dep = [local(dep.at[:, :, r, :], dpt.at[r], sem_dep) for r in range(RB)]
    small = [
        local(src, dst, sem_small.at[i])
        for i, (src, dst) in enumerate(((obs_h, obs), (err_h, err), (pen_h, pen), (fst_h, fst), (fwt_h, fwt)))
    ]
    for c in stage_x + stage_ae:
        c.start()

    barrier = pltpu.get_barrier_semaphore()

    def hello(to, sem=barrier):
        pl.semaphore_signal(sem, inc=1, device_id=to, device_id_type=MESH)

    for d in FAR + (0,):
        for i in range(4):
            if d or i:
                hello((lax.rem(tm + d, 8), base + lax.rem(lat + i, 4), lon))
    next_x, last_x = lax.rem(base + 4, 16), lax.rem(base + 12, 16)
    either, not_both = (pair == 1) | (core == 1), (pair == 0) | (core == 0)
    for to_lat, there in (
        (next_x, either),
        (next_x + 1, core == 1),
        (next_x + 2, pair == 1),
        (last_x + 1, pair == 0),
        (last_x + 2, core == 0),
        (last_x + 3, not_both),
    ):

        @pl.when(there)
        def _(to_lat=to_lat):
            for d in FAR + (0,):
                hello((lax.rem(tm + d, 8), to_lat, lon))

    for c in stage_dep + small:
        c.start()
    east, west = lax.rem(lon + 1, 4), lax.rem(lon + 3, 4)
    to_east, to_west = (tm, lat, east), (tm, lat, west)
    east_later, west_later = lon < 2, (lon == 0) | (lon == 3)
    earlier = (lon > 0).astype(jnp.int32) + (lon == 2).astype(jnp.int32)
    lane16 = lax.broadcasted_iota(jnp.int32, (LEV, 128), 1)
    lane8 = lax.broadcasted_iota(jnp.int32, (8, 128), 1)

    local(xt, xt, sem_x).wait()
    own = ae.at[:, pl.ds(8, RB), :, pl.ds(0, COLS)]
    local(own, own, sem_ae).wait()
    for f in range(3):
        packed = jnp.zeros((LEV, 128), jnp.float32)
        for r in range(RB):
            field = xt.at[r] if f == 0 else ae.at[f - 1, 8 + r]
            edge = jnp.where(lane16 >= 122, field[:, 256:384], field[:, 0:128])
            rolled = pltpu.roll(edge, 12 * r + 6, 1)
            packed = jnp.where((lane16 >= 12 * r) & (lane16 < 12 * r + 12), rolled, packed)
        pks[f] = packed

    crossing = 2 + either.astype(jnp.int32) + not_both.astype(jnp.int32)
    pl.semaphore_wait(barrier, 31 + 8 * crossing + earlier)
    pl.when(east_later)(lambda: hello(to_east))
    pl.when(west_later)(lambda: hello(to_west))
    pl.when(not_(east_later))(lambda: hello(to_east, answer))
    pl.when(not_(west_later))(lambda: hello(to_west, answer))

    def owners(p):
        own = base + 2 * p + pair
        return (
            (1, 2, own, None),
            (0, 0, lax.rem(own + 1 + 2 * pair, 16), chip_up),
            (2, 4, lax.rem(own + 13 + 2 * pair, 16), chip_down),
        )

    packed_coefs = pks.at[pl.ds(1, 2)]
    sent_lp = (
        remote(packed_coefs, lp.at[2], lp_send.at[0], lp_recv.at[2], (tm, below, east)),
        remote(packed_coefs, lp.at[1], lp_send.at[1], lp_recv.at[1], (tm, lat, east)),
        remote(packed_coefs, lp.at[0], lp_send.at[2], lp_recv.at[0], (tm, above, east)),
    )

    def send_edges(side, to_lon):
        def to_tm_of(d, _):
            to_tm = lax.rem(tm + d, 8)
            for p in range(2):
                for pos, group, to, there in owners(p):
                    copy = remote(
                        pks.at[pl.ds(0, 1), 2 * to_tm + p, :],
                        ws.at[side, pl.ds(group + core, 1), tm, :],
                        ws_send.at[pos],
                        ws_recv.at[side, pos],
                        (to_tm, to, to_lon),
                    )
                    if there is None:
                        copy.start()
                    else:
                        pl.when(there)(lambda copy=copy: copy.start())
            return 0

        lax.fori_loop(0, 8, to_tm_of, 0)
        for p in range(2):
            for pos, group, to, there in owners(p):
                copy = remote(
                    pks.at[pl.ds(1, 2), 2 * tm + p, :],
                    cw.at[side, :, group + core, :],
                    cw_send.at[pos],
                    cw_recv.at[side, pos],
                    (tm, to, to_lon),
                )
                if there is None:
                    copy.start()
                else:
                    pl.when(there)(lambda copy=copy: copy.start())
        if side == 0:
            sent_lp[1].start()
            pl.when(lat_down)(lambda: sent_lp[0].start())
            pl.when(lat_up)(lambda: sent_lp[2].start())

    pl.when(not_(east_later))(lambda: send_edges(0, east))
    pl.when(not_(west_later))(lambda: send_edges(1, west))

    def start_to(to, myself, src, dst, send, recv):
        copy = remote(src, dst, send, recv, to)
        if myself is None:
            copy.start()
            return
        pl.when(jnp.logical_not(myself))(lambda: copy.start())
        pl.when(myself)(lambda: local(src, dst, recv).start())

    diagonal = core == pair

    for d in FAR + (0,):
        to_tm = lax.rem(tm + d, 8)
        for e in range(2):
            p = lax.rem(pair + 1 + e, 2)
            start_to(
                (to_tm, base + 2 * p + pair, lon),
                diagonal if d == 0 and e == 1 else None,
                inc.at[2 * to_tm + p],
                s0.at[pl.ds(16 + 8 * core, RB), tm, pl.ds(0, COLS)],
                a_send,
                a_recv.at[2 * d + core],
            )
    for e in range(2):
        p = lax.rem(pair + 1 + e, 2)
        for pos, group, to, there in owners(p):
            for a, src in enumerate((adv, dif)):
                args = (src.at[2 * tm + p], cl.at[a, group + core, :, pl.ds(0, COLS)], cl_send.at[pos], cl_recv.at[pos])
                myself = to == lat if e == 1 else None
                if there is None:
                    start_to((tm, to, lon), myself, *args)
                else:
                    pl.when(there)(lambda to=to, myself=myself, args=args: start_to((tm, to, lon), myself, *args))

    def rows_of(first):
        return ae.at[:, pl.ds(first, 4), :, pl.ds(0, COLS)]

    sent_e = (
        remote(rows_of(8), rows_of(16), e_send.at[0], e_recv.at[0], band_down),
        remote(rows_of(12), rows_of(4), e_send.at[1], e_recv.at[1], band_up),
    )
    pl.when(lat_down)(lambda: sent_e[0].start())
    pl.when(lat_up)(lambda: sent_e[1].start())

    for c in small:
        c.wait()
    sub = lax.broadcasted_iota(jnp.int32, (8, WIDE), 0)
    for s in range(STEPS):
        t = sub * STEPS + s
        total = jnp.where(t == K * STEPS // 2, -1.0, 0.0)
        for j in range(24):
            total = total + jnp.where(t == fst[j], fwt[j], 0.0)
        cv[s] = total

    for there, first in ((has_down, 0), (has_up, 4)):

        @pl.when(not_(there))
        def _(first=first):
            s0[8 * first : 8 * first + 16] = jnp.zeros((16, 8, WIDE), jnp.float32)
            cl[:, first : first + 2] = jnp.zeros((2, 2, 8, COLS), jnp.float32)
            cw[:, :, first : first + 2] = jnp.zeros((2, 2, 2, 128), jnp.float32)
            ws[:, first : first + 2] = jnp.zeros((2, 2, 8, 128), jnp.float32)

    for there, first, i in ((lat_down, 4, 0), (lat_up, 16, 1)):

        @pl.when(not_(there))
        def _(first=first, i=i):
            ae[:, first : first + 4] = jnp.zeros((2, 4, LEV, WIDE), jnp.float32)
            lr[i] = jnp.zeros((5, LEV, COLS), jnp.float32)
            pr[2 * i] = jnp.zeros((LEV, 128), jnp.float32)

    for row in (2, 3, 20, 21):
        ae[:, row] = jnp.zeros((2, LEV, WIDE), jnp.float32)
    u0[...] = jnp.zeros(u0.shape, jnp.float32)
    u1[...] = jnp.zeros(u1.shape, jnp.float32)

    sides = ((has_down, 16, 32, 0, owner_down), (has_up, 20, 4, 1, owner_up))

    def pass_on(d):
        k = lax.rem(tm + 8 - d, 8)
        for e in range(2):
            block = s0.at[pl.ds(16 + 8 * e, RB), k, pl.ds(0, COLS)]
            local(block, block, a_recv.at[2 * d + e]).wait()
        for there, start, at_row, i, to in sides:
            copy = remote(
                s0.at[pl.ds(start, 12), k, pl.ds(0, COLS)],
                s0.at[pl.ds(at_row, 12), k, pl.ds(0, COLS)],
                h_send.at[i],
                h_recv.at[i],
                to,
            )
            pl.when(there)(lambda copy=copy: copy.start())

    for d in NEAR:
        pass_on(d)

    pl.when(lon != 2)(lambda: pl.semaphore_wait(answer, 2 - earlier))
    pl.when(east_later)(lambda: send_edges(0, east))
    pl.when(west_later)(lambda: send_edges(1, west))

    local(dpt, dpt, sem_dep).wait()
    us = (u0, u1)
    for r in range(RB):
        u0[8 + r, :, 0:COLS] = dpt[r, STEPS - 1]

    def dep_step(n):
        u, new = us[(n + 1) % 2], us[n % 2]

        def moved(r):
            v, a, d = u[r], ae[0, r], ae[1, r]
            p = pltpu.roll(a * v, WIDE - 1, 1)
            return (1.0 - a - 2.0 * d) * v + p + (ae[1, r + 1] * u[r + 1] + ae[1, r - 1] * u[r - 1])

        def outer(r, _):
            new[r] = moved(r)
            return 0

        def inner(r, _):
            fresh = moved(r)
            new[r, :, 0:COLS] = fresh[:, 0:COLS] + dpt[r - 8, STEPS - 1 - n]
            new[r, :, COLS:WIDE] = fresh[:, COLS:WIDE]
            return 0

        lax.fori_loop(8 - n, 8, outer, 0, unroll=True)
        lax.fori_loop(8, 16, inner, 0, unroll=True)
        lax.fori_loop(16, 16 + n, outer, 0, unroll=True)

    def tile_of(packed, r):
        return jnp.where(lane16 >= 122, pltpu.roll(packed, 122 - 12 * r, 1), 0.0)

    def put_tiles(i, rows, shift):
        for a in range(2):
            for r in rows:
                ae[a, r, :, COLS:WIDE] = tile_of(lp[i, a], r - shift)

    sent_lp[1].wait_recv()
    put_tiles(1, range(8, 16), 8)

    @pl.when(lat_up)
    def _():
        sent_e[0].wait_recv()
        sent_lp[0].wait_recv()
        put_tiles(2, range(16, 20), 16)

    @pl.when(lat_down)
    def _():
        sent_e[1].wait_recv()
        sent_lp[2].wait_recv()
        put_tiles(0, range(4, 8), 0)

    for n in range(1, STEPS):
        dep_step(n)
    us_end = us[1]
    packed = jnp.zeros((LEV, 128), jnp.float32)
    for i in range(18):
        rolled = pltpu.roll(us_end[3 + i, :, COLS:WIDE], 5 * i + 5, 1)
        packed = jnp.where((lane16 >= 5 * i) & (lane16 < 5 * i + 5), rolled, packed)
    ps[...] = packed
    sent_p = (
        remote(ps, pr.at[2], p_send.at[0], p_recv.at[2], (tm, below, west)),
        remote(ps, pr.at[1], p_send.at[1], p_recv.at[1], to_west),
        remote(ps, pr.at[0], p_send.at[2], p_recv.at[0], (tm, above, west)),
    )
    sent_r = (
        remote(us_end.at[pl.ds(3, 5), :, pl.ds(0, COLS)], lr.at[1], r_send.at[0], r_recv.at[0], band_down),
        remote(us_end.at[pl.ds(16, 5), :, pl.ds(0, COLS)], lr.at[0], r_send.at[1], r_recv.at[1], band_up),
    )
    sent_p[1].start()

    @pl.when(lat_down)
    def _():
        sent_p[0].start()
        sent_r[0].start()

    @pl.when(lat_up)
    def _():
        sent_p[2].start()
        sent_r[1].start()

    def arrived(pos):
        block = cl.at[:, pl.ds(0, 2), :, pl.ds(0, COLS)]
        local(block, block, cl_recv.at[pos]).wait()
        rows = pks.at[0, pl.ds(0, 4)]
        for side in range(2):
            local(rows, rows, cw_recv.at[side, pos]).wait()

    arrived(1)
    pl.when(has_down)(lambda: arrived(0))
    pl.when(has_up)(lambda: arrived(2))
    from_west = lax.rem(lane8, 12) < 6
    halo_lanes = (lane8 < 6) | (lane8 >= 122)

    def widen(g, _):
        edges = []
        for a in range(2):
            parts = [jnp.broadcast_to(cw[side, a, pl.ds(g, 1), :], (8, 128)) for side in range(2)]
            edges.append(jnp.where(from_west, *parts))
        for r in range(RB):
            a = jnp.broadcast_to(cl[0, g, r : r + 1, :], (8, COLS))
            d = jnp.broadcast_to(cl[1, g, r : r + 1, :], (8, COLS))
            at, dt = (jnp.where(halo_lanes, pltpu.roll(x, 122 - 12 * r, 1), 0.0) for x in edges)
            for cols, x, y in ((slice(0, COLS), a, d), (slice(COLS, WIDE), at, dt)):
                ab[8 * g + r, :, cols] = x
                db[8 * g + r, :, cols] = y
                kb[8 * g + r, :, cols] = 1.0 - x - 2.0 * y
        return 0

    lax.fori_loop(0, 6, widen, 0)

    def edges_in(pos):
        rows = ws.at[0, pl.ds(0, 2)]
        for side in range(2):
            local(rows, rows, ws_recv.at[side, pos]).wait()

    edges_in(1)
    for there, rows, i, pos in ((has_up, pl.ds(32, 12), 0, 2), (has_down, pl.ds(4, 12), 1, 0)):
        block = s0.at[rows, :, pl.ds(0, COLS)]

        @pl.when(there)
        def _(block=block, i=i, pos=pos):
            local(block, block, h_recv.at[i]).wait()
            edges_in(pos)

    def unpack(g, _):
        mine = jnp.where(from_west, ws[0, g], ws[1, g])
        for r in range(RB):
            rolled = pltpu.roll(mine, 122 - 12 * r, 1)
            s0[8 * g + r, :, COLS:WIDE] = jnp.where(halo_lanes, rolled, 0.0)
        return 0

    lax.fori_loop(0, 6, unpack, 0)

    for s in range(STEPS):
        now, later = states[s], states[s + 1]

        def forward(i, _, now=now, later=later, s=s):
            r = 5 + s + 2 * i
            x = now[pl.ds(r - 1, 4)]
            rows = pl.ds(r, 2)
            centre = x[1:3]
            moved = pltpu.roll(centre, 1, 2)
            later[rows] = kb[rows] * centre + ab[rows] * moved + db[rows] * (x[2:4] + x[0:2])
            return 0

        lax.fori_loop(0, 19 - s, forward, 0, unroll=True)

    weight_obs, weight_err, weight_pen = obs[level], err[level], pen[level]

    def filtered(i, _):
        rows = pl.ds(11 + 2 * i, 2)
        total = cv[0] * s0[rows]
        for s in range(1, STEPS):
            total = total + cv[s] * states[s][rows]
        summed = weight_pen * jnp.sum(total, axis=1, keepdims=True)
        force[rows] = jnp.broadcast_to(summed, (2, 8, WIDE))
        return 0

    lax.fori_loop(0, 13, filtered, 0, unroll=True)

    first = lax.broadcasted_iota(jnp.int32, (2, 8, WIDE), 1) == 0
    final = lax.broadcasted_iota(jnp.int32, (2, 8, WIDE), 1) == 7

    def start(i, _):
        rows = pl.ds(10 + 2 * i, 2)
        m = s0[rows] - jnp.where(first, 0.0, pltpu.roll(s6[rows], 1, 1))
        mis[rows] = jnp.where(first, m, weight_err * m)
        v0[rows] = jnp.where(final, 0.0, -weight_err * pltpu.roll(m, 7, 1))
        return 0

    lax.fori_loop(0, 14, start, 0, unroll=True)

    vs = (v0, v1)
    for n in range(1, STEPS + 1):
        s = STEPS - n
        now, later = vs[(n + 1) % 2], vs[n % 2]

        def backward(i, _, now=now, later=later, s=s, n=n):
            r = 10 + n + 2 * i
            rows = pl.ds(r, 2)
            v = now[pl.ds(r - 1, 4)]
            spread = db[pl.ds(r - 1, 4)] * v
            centre = v[1:3]
            carried = pltpu.roll(ab[rows] * centre, WIDE - 1, 2)
            forcing = weight_obs * states[s][rows] + cv[s] * force[rows]
            fresh = forcing + (kb[rows] * centre + carried + (spread[2:4] + spread[0:2]))
            if s == 0:
                fresh = fresh + mis[rows]
            later[rows] = fresh
            return 0

        if s > 0:
            lax.fori_loop(0, 14 - n, backward, 0, unroll=True)
            continue
        for half in range(2):
            lax.fori_loop(4 * half, 4 * half + 4, backward, 0, unroll=True)
            for d in FAR + (0,):
                to_tm = lax.rem(tm + d, 8)
                to = base + 2 * core + half
                start_to(
                    (to_tm, to, lon),
                    to == lat if d == 0 else None,
                    later.at[pl.ds(16 + 8 * half, RB), to_tm, pl.ds(0, COLS)],
                    gr.at[level],
                    g_send,
                    g_recv,
                )

    level16 = lax.broadcasted_iota(jnp.int32, (LEV, COLS), 0)
    obs_all = jnp.zeros((LEV, COLS), jnp.float32)
    for lv in range(LEV):
        obs_all = jnp.where(level16 == lv, obs[lv], obs_all)
    sent_p[1].wait_recv()

    @pl.when(lat_up)
    def _():
        sent_r[0].wait_recv()
        sent_p[0].wait_recv()

    @pl.when(lat_down)
    def _():
        sent_r[1].wait_recv()
        sent_p[2].wait_recv()

    for r in range(RB):
        total = us_end[8 + r, :, 0:COLS]
        parts = [(1, 5 + r)]
        if r < 5:
            total = total + lr[0, r]
            parts.append((0, 13 + r))
        if r >= 3:
            total = total + lr[1, r - 3]
            parts.append((2, r - 3))
        shares = [pltpu.roll(pr[i], (123 - 5 * row) % 128, 1) for i, row in parts]
        edge = jnp.where(lane16 >= 123, sum(shares[1:], shares[0]), 0.0)
        total = jnp.concatenate([total[:, 0:256], total[:, 256:384] + edge], axis=1)
        moved_back[:, r, :] = obs_all * total

    def drain(whole, fewer, sem):
        pl.when(diagonal)(lambda: local(fewer, fewer, sem).wait())
        pl.when(not_(diagonal))(lambda: local(whole, whole, sem).wait())

    sixteen, fifteen = (s1.at[pl.ds(0, n), :, pl.ds(0, COLS)] for n in (16, 15))
    drain(sixteen, fifteen, a_send)
    drain(s1.at[pl.ds(0, 4), :, pl.ds(0, COLS)], s1.at[pl.ds(0, 2), :, pl.ds(0, COLS)], cl_send.at[1])

    def edges_out(pos):
        rows = lp.at[0]
        local(rows, rows, ws_send.at[pos]).wait()
        rows = pks.at[0, pl.ds(0, 8)]
        local(rows, rows, cw_send.at[pos]).wait()
        if pos != 1:
            myself = not_(diagonal) & ((pair == 0) if pos == 0 else (pair == 1))
            for flag, n in ((myself, 2), (not_(myself), 4)):
                block = s1.at[pl.ds(0, n), :, pl.ds(0, COLS)]
                pl.when(flag)(lambda block=block: local(block, block, cl_send.at[pos]).wait())

    edges_out(1)
    pl.when(chip_up)(lambda: edges_out(0))
    pl.when(chip_down)(lambda: edges_out(2))
    for i, there in enumerate((has_down, has_up)):
        block = s1.at[pl.ds(4, 12), :, pl.ds(0, COLS)]
        pl.when(there)(lambda i=i, block=block: local(block, block, h_send.at[i]).wait())
    sent_p[1].wait_send()
    sent_lp[1].wait_send()
    for i, there in enumerate((lat_down, lat_up)):

        @pl.when(there)
        def _(i=i):
            for c in (sent_e[i], sent_lp[2 * i], sent_r[i], sent_p[2 * i]):
                c.wait_send()

    local(gr, gr, g_recv).wait()
    drain(sixteen, fifteen, g_send)


def body(increments, advection, diffusion, departures, obs, err, pen, steps, weights):
    f32 = jnp.float32
    big = pltpu.VMEM((ROWS, 8, WIDE), f32)
    dma = pltpu.SemaphoreType.DMA
    scratch = [pltpu.SMEM((LEV,), f32)] * 3 + [pltpu.SMEM((24,), jnp.int32), pltpu.SMEM((24,), f32)]
    scratch += [big] * 14 + [pltpu.VMEM((STEPS, 8, WIDE), f32)]
    scratch += [
        pltpu.VMEM((2, 6, 8, COLS), f32),
        pltpu.VMEM((2, 2, 6, 128), f32),
        pltpu.VMEM((2, 24, LEV, WIDE), f32),
        pltpu.VMEM((2, 6, 8, 128), f32),
        pltpu.VMEM((3, LEV, 128), f32),
        pltpu.VMEM((3, 2, LEV, 128), f32),
        pltpu.VMEM((RB, LEV, COLS), f32),
        pltpu.VMEM((RB, STEPS, LEV, COLS), f32),
        pltpu.VMEM((24, LEV, WIDE), f32),
        pltpu.VMEM((24, LEV, WIDE), f32),
        pltpu.VMEM((2, 5, LEV, COLS), f32),
        pltpu.VMEM((LEV, 128), f32),
        pltpu.VMEM((3, LEV, 128), f32),
    ]
    scratch += [pltpu.SemaphoreType.REGULAR, dma, dma, dma, dma((5,))]
    scratch += [dma, dma((16,)), dma((3,)), dma((2, 3)), dma((3,)), dma((3,)), dma((3,)), dma((2, 3))]
    scratch += [dma((2,)), dma((2,)), dma((2,)), dma((2,)), dma((3,)), dma((3,)), dma((2,)), dma((2,)), dma((3,)), dma((3,)), dma, dma]
    block = OUT((LEV, RB, COLS), f32)
    own, moved_back = pl.pallas_call(
        kernel,
        out_shape=(block, block),
        in_specs=[pl.BlockSpec(memory_space=pl.ANY)] * 9,
        out_specs=(pl.BlockSpec(memory_space=pltpu.VMEM),) * 2,
        scratch_shapes=scratch,
        compiler_params=pltpu.CompilerParams(
            collective_id=0, has_side_effects=True, vmem_limit_bytes=VMEM_KIB * 1024
        ),
        name="gradient",
    )(increments[0], advection, diffusion, departures[0], obs, err, pen, steps, weights)
    return (own - moved_back)[None]


def solution(mesh):
    return jax.shard_map(
        body,
        mesh=mesh,
        in_specs=(
            P("tm", None, "lat", "lon"),
            P(None, "lat", "lon"),
            P(None, "lat", "lon"),
            P("tm", None, None, "lat", "lon"),
            P(),
            P(),
            P(),
            P(),
            P(),
        ),
        out_specs=P("tm", None, "lat", "lon"),
        check_vma=False,
    )
```

time: 40.6 us -> 36.4 us (0.90); the launches traced: 39.9 us -> 36.2 us
  Pallas kernels: 38.3 us -> 35.5 us
  local copies, waits for them, and re-layouts: 1.62 us -> 0 us
  other arithmetic: 0 us -> 0.7 us
    pallas_call x1, Pallas kernels: 38.3 us -> 35.5 us  [body(): pl.pallas_call(kernel, out_shape=(block, block), in_specs=[pl.BlockSpec(m...]
    unnamed x1 -> x0, local copies, waits for them, and re-layouts: 1.62 us -> none
    broadcast_in_dim x0 -> x1, other arithmetic: none -> 0.7 us  [body(): return (own - moved_back)[None]]
where the time goes in v3:
time: 36.4 us; the launch traced here: 36.2 us
  Pallas kernels  35.5 us (98%)
  other arithmetic  0.7 us (2%)
    pallas_call x1, Pallas kernels, body(): pl.pallas_call(kernel, out_shape=(block, block), in_specs=[pl.BlockSpec(m...  35.5 us

profile of v3, /device:TPU:1, one launch (start us, length us, event | category | flops | bytes accessed | tf_op | source)
XLA Modules:
  0.0 36.2 jit_solution(653633990307984250)
XLA Ops:
  0.0 35.5 %gradient.1 = (f32[16,8,384]{2,1,0:T(8,128)S(1)}, f32[16,8,384]{2,1,0:T(8,128)S(1)}) custom-call(f32[16,8,384]{2,1,0:T(8,128)} %bitcast.5, f32[16,8,384]{2,1,0:T(8,128)} %adv.1, f32[16,8,384]{2,1,0:T(8,128)} %dif.1, f32[6,16,8,384]{3,2,1,0:T(8,128)} %bitcast.4, f32[16]{0:T(128)} %obs_h.1, f32[16]{0:T(128)} %err_h.1, f32[16]{0:T(128)} %pen_h.1, s32[24]{0:T(128)} %fst_h.1, ...), custom_call_target="tpu_custom_call" | custom-call | tf_op jit(solution)/shard_map/gradient/pallas_call | solution.py:576
  35.5 0.7 %subtract_bitcast_fusion = f32[1,16,8,384]{3,2,1,0:T(8,128)} fusion(f32[16,8,384]{2,1,0:T(8,128)S(1)} %get-tuple-element.7, f32[16,8,384]{2,1,0:T(8,128)S(1)} %get-tuple-element.8), kind=kLoop, calls=%fused_computation | loop fusion | flops 49152 | bytes 589824 | tf_op jit(solution)/shard_map/broadcast_in_dim | solution.py:587

commit v4 on v3

--- a/solution.py
+++ b/solution.py
@@ -171,8 +171,8 @@
             pl.when(lat_down)(lambda: sent_lp[0].start())
             pl.when(lat_up)(lambda: sent_lp[2].start())
 
-    pl.when(not_(east_later))(lambda: send_edges(0, east))
-    pl.when(not_(west_later))(lambda: send_edges(1, west))
+    pl.when(lon == 3)(lambda: send_edges(0, east))
+    pl.when((lon == 1) | (lon == 2))(lambda: send_edges(1, west))
 
     def start_to(to, myself, src, dst, send, recv):
         copy = remote(src, dst, send, recv, to)
@@ -196,6 +196,8 @@
                 a_send,
                 a_recv.at[2 * d + core],
             )
+    pl.when(lon == 2)(lambda: send_edges(0, east))
+
     for e in range(2):
         p = lax.rem(pair + 1 + e, 2)
         for pos, group, to, there in owners(p):

time: 36.4 us -> 36.3 us (level)
  no operation moved by 1% of the time
where the time goes in v4:
time: 36.3 us; the launch traced here: 36.1 us
  Pallas kernels  35.4 us (98%)
  other arithmetic  0.7 us (2%)
    pallas_call x1, Pallas kernels, body(): pl.pallas_call(kernel, out_shape=(block, block), in_specs=[pl.BlockSpec(m...  35.4 us

profile of v4, /device:TPU:1, one launch (start us, length us, event | category | flops | bytes accessed | tf_op | source)
XLA Modules:
  0.0 36.1 jit_solution(16495420567252877077)
XLA Ops:
  0.0 35.4 %gradient.1 = (f32[16,8,384]{2,1,0:T(8,128)S(1)}, f32[16,8,384]{2,1,0:T(8,128)S(1)}) custom-call(f32[16,8,384]{2,1,0:T(8,128)} %bitcast.5, f32[16,8,384]{2,1,0:T(8,128)} %adv.1, f32[16,8,384]{2,1,0:T(8,128)} %dif.1, f32[6,16,8,384]{3,2,1,0:T(8,128)} %bitcast.4, f32[16]{0:T(128)} %obs_h.1, f32[16]{0:T(128)} %err_h.1, f32[16]{0:T(128)} %pen_h.1, s32[24]{0:T(128)} %fst_h.1, ...), custom_call_target="tpu_custom_call" | custom-call | tf_op jit(solution)/shard_map/gradient/pallas_call | solution.py:578
  35.4 0.7 %subtract_bitcast_fusion = f32[1,16,8,384]{3,2,1,0:T(8,128)} fusion(f32[16,8,384]{2,1,0:T(8,128)S(1)} %get-tuple-element.7, f32[16,8,384]{2,1,0:T(8,128)S(1)} %get-tuple-element.8), kind=kLoop, calls=%fused_computation | loop fusion | flops 49152 | bytes 589824 | tf_op jit(solution)/shard_map/broadcast_in_dim | solution.py:589
